TPU v7x, 32 devices: a whole 2x2x4 slice. The times are simulated.
32 devices in a mesh: dp: 8 (over y, x, core), mp: 4 (over z).
Axes of the slice: x: 2, y: 2, z: 4, core: 2. Of those that a mesh axis runs over, the one named last changes fastest.
Arguments:
- tokens: bfloat16 [8, 1024, 768], P('dp', 'mp'), may hold values from -6 to 6
- doc_starts: int32 [8, 2], P('dp'), may hold values from 0 to 1023, as said below
- query_proj: bfloat16 [768, 768], replicated, may hold values from -0.21875 to 0.21875
- key_proj: bfloat16 [768, 768], replicated, may hold values from -0.21875 to 0.21875
- value_proj: bfloat16 [768, 768], replicated, may hold values from -0.21875 to 0.21875
- query_bias: float32 [768], replicated, may hold values from -1.2 to 1.2
- key_bias: float32 [768], replicated, may hold values from -1.2 to 1.2
- value_bias: float32 [768], replicated, may hold values from -1.2 to 1.2
- output_proj: bfloat16 [768, 768], replicated, may hold values from -1.75 to 1.75
- output_bias: float32 [768], replicated, may hold values from -1.2 to 1.2
- attn_gain: float32 [768], replicated, may hold values from 0.5 to 1.5
- attn_shift: float32 [768], replicated, may hold values from -1.2 to 1.2
- up_proj: bfloat16 [768, 3072], P(None, 'mp'), may hold values from -0.21875 to 0.21875
- up_bias: float32 [3072], P('mp'), may hold values from -1.2 to 1.2
- down_proj: bfloat16 [3072, 768], P('mp'), may hold values from -0.109375 to 0.109375
- down_bias: float32 [768], replicated, may hold values from -1.2 to 1.2
- ffn_gain: float32 [768], replicated, may hold values from 0.5 to 1.5
- ffn_shift: float32 [768], replicated, may hold values from -1.2 to 1.2
- cotangent: bfloat16 [8, 1024, 768], P('dp', 'mp'), may hold values from -6 to 6
Outputs:
- layer_out: bfloat16 [8, 1024, 768], P('dp', 'mp')
- input_grad: bfloat16 [8, 1024, 768], P('dp', 'mp')
- query_proj_grad: float32 [768, 768], replicated
- key_proj_grad: float32 [768, 768], replicated
- value_proj_grad: float32 [768, 768], replicated
- query_bias_grad: float32 [768], replicated
- key_bias_grad: float32 [768], replicated
- value_bias_grad: float32 [768], replicated
- output_proj_grad: float32 [768, 768], replicated
- output_bias_grad: float32 [768], replicated
- attn_gain_grad: float32 [768], replicated
- attn_shift_grad: float32 [768], replicated
- up_proj_grad: float32 [768, 3072], P(None, 'mp')
- up_bias_grad: float32 [3072], P('mp')
- down_proj_grad: float32 [3072, 768], P('mp')
- down_bias_grad: float32 [768], replicated
- ffn_gain_grad: float32 [768], replicated
- ffn_shift_grad: float32 [768], replicated
Inputs may be any that keep to these rules, and one draw needn't show every extreme that they name: doc_starts[r, 0] = 0 and for d >= 1 doc_starts[r, d] lies in [d * 512 + 1, (d + 1) * 512); document d of row r runs from its start to the next start (or 1024) minus one.
All inputs are finite; a program needn't handle non-finite values.
Results may differ from a plain program's by a relative error of at most 0.025.
Values may be sent and summed in bfloat16 or wider, within the bound.
A program may use at most 256 MiB of HBM per device.

v0:
```python
from functools import partial
import math

import jax
import jax.numpy as jnp
from jax import lax
from jax.sharding import PartitionSpec as P

HEADS = 12
HD = 64
SEQ = 1024
BLOCK = 64
DOCS = 2


highest = lax.Precision.HIGHEST


def layer_norm(inputs, norm_gain, norm_shift):
    center = inputs - jnp.mean(inputs, axis=-1, keepdims=True)
    spread = jnp.mean(center * center, axis=-1, keepdims=True)
    return center * lax.rsqrt(spread + 1e-05) * norm_gain + norm_shift


def doc_layout(starts):
    places = jnp.arange(SEQ, dtype=jnp.int32)
    inside = (starts[None, :] <= places[:, None]).astype(jnp.int32)
    number = jnp.sum(inside, axis=1) - 1
    picked = jnp.arange(DOCS, dtype=jnp.int32)[None, :] == number[:, None]
    ending = jnp.concatenate([starts[1:], jnp.full((1,), SEQ, jnp.int32)])
    opened = jnp.sum(jnp.where(picked, starts[None, :], 0), axis=1)
    closed = jnp.sum(jnp.where(picked, ending[None, :], 0), axis=1)
    angles = (
        (places - opened).astype(jnp.float32)
        * (0.5 * math.pi)
        / (closed - opened).astype(jnp.float32)
    )
    return (number, jnp.cos(angles), jnp.sin(angles))


def rowwise(left, right):
    return jnp.einsum("rlk,kn->rln", left, right, preferred_element_type=jnp.float32)


def features(pre_act, cos_part, sin_part):
    batch_rows, length = (pre_act.shape[0], pre_act.shape[1])
    head_vals = jax.nn.relu(pre_act).reshape(batch_rows, length, HEADS, HD)
    combined = jnp.concatenate(
        [head_vals * cos_part[:, :, None, None], head_vals * sin_part[:, :, None, None]], axis=3
    )
    return combined.astype(jnp.bfloat16).reshape(batch_rows, length // BLOCK, BLOCK, HEADS, 2 * HD)


def features_back(pre_act, cos_part, sin_part, feat_grads):
    batch_rows, length = (pre_act.shape[0], pre_act.shape[1])
    grads_flat = feat_grads.reshape(batch_rows, length, HEADS, 2 * HD)
    head_grad = (
        grads_flat[..., :HD] * cos_part[:, :, None, None]
        + grads_flat[..., HD:] * sin_part[:, :, None, None]
    )
    return jnp.where(pre_act > 0, head_grad.reshape(batch_rows, length, HEADS * HD), 0.0)


def block_masks(number):
    batch_rows = number.shape[0]
    doc_ids = number.reshape(batch_rows, -1, BLOCK)
    within = jnp.arange(BLOCK, dtype=jnp.int32)
    allowed = (within[:, None] >= within[None, :])[None, None] & (
        doc_ids[..., :, None] == doc_ids[..., None, :]
    )
    lastdoc = doc_ids[..., -1]
    in_last = doc_ids == lastdoc[..., None]
    block_ids = jnp.arange(doc_ids.shape[1], dtype=jnp.int32)
    linked = (
        (block_ids[None, :] <= block_ids[:, None])[None]
        & (lastdoc[:, None, :] == lastdoc[:, :, None])
    ).astype(jnp.float32)
    prevdoc = jnp.concatenate([jnp.full((batch_rows, 1), -1, jnp.int32), lastdoc[:, :-1]], axis=1)
    carried = (doc_ids == prevdoc[..., None]).astype(jnp.float32)
    return (allowed, in_last, linked, carried)


def shift_blocks(array):
    return jnp.concatenate([jnp.zeros_like(array[:, :1]), array[:, :-1]], axis=1)


def unshift_blocks(array):
    return jnp.concatenate([array[:, 1:], jnp.zeros_like(array[:, :1])], axis=1)


def block_states(key_feats, values, in_last, linked):
    masked_keys = jnp.where(in_last[..., None, None], key_feats, jnp.zeros_like(key_feats))
    contrib = jnp.einsum(
        "rnjhf,rnjhd->rnhfd", masked_keys, values, preferred_element_type=jnp.float32
    )
    key_sums = jnp.sum(masked_keys.astype(jnp.float32), axis=2)
    states = jnp.einsum("rcb,rbhfd->rchfd", linked, contrib, precision=highest)
    state_sums = jnp.einsum("rcb,rbhf->rchf", linked, key_sums, precision=highest)
    return (masked_keys, shift_blocks(states), shift_blocks(state_sums))


def attend(query_feats, key_feats, values, block_info):
    allowed, in_last, linked, carried = block_info
    scores = jnp.einsum(
        "rnihf,rnjhf->rnhij", query_feats, key_feats, preferred_element_type=jnp.float32
    )
    scores = jnp.where(allowed[:, :, None], scores, 0.0)
    local_part = jnp.einsum(
        "rnhij,rnjhd->rnihd",
        scores.astype(jnp.bfloat16),
        values,
        preferred_element_type=jnp.float32,
    )
    score_sums = jnp.sum(scores, axis=4).transpose(0, 1, 3, 2)
    masked_keys, prior_states, prior_sums = block_states(key_feats, values, in_last, linked)
    remote = (
        jnp.einsum(
            "rnihf,rnhfd->rnihd",
            query_feats,
            prior_states.astype(jnp.bfloat16),
            preferred_element_type=jnp.float32,
        )
        * carried[..., None, None]
    )
    remote_den = (
        jnp.einsum(
            "rnihf,rnhf->rnih", query_feats.astype(jnp.float32), prior_sums, precision=highest
        )
        * carried[..., None]
    )
    numerator = local_part + remote
    raw_den = score_sums + remote_den
    context = numerator / jnp.maximum(raw_den, 1.0)[..., None]
    return (context, numerator, raw_den)


def attend_back(query_feats, key_feats, values, block_info, numerator, raw_den, context_grad):
    allowed, in_last, linked, carried = block_info
    denominator = jnp.maximum(raw_den, 1.0)
    grad_vals = context_grad.astype(jnp.float32)
    numer_grad = (grad_vals / denominator[..., None]).astype(jnp.bfloat16)
    den_grad = -jnp.sum(grad_vals * numerator, axis=-1) / (denominator * denominator)
    den_grad = jnp.where(raw_den > 1.0, den_grad, 0.0)
    scores = jnp.einsum(
        "rnihf,rnjhf->rnhij", query_feats, key_feats, preferred_element_type=jnp.float32
    )
    scores_low = jnp.where(allowed[:, :, None], scores, 0.0).astype(jnp.bfloat16)
    score_grad = jnp.einsum(
        "rnihd,rnjhd->rnhij", numer_grad, values, preferred_element_type=jnp.float32
    )
    score_grad = score_grad + den_grad.transpose(0, 1, 3, 2)[..., None]
    score_grad = jnp.where(allowed[:, :, None], score_grad, 0.0).astype(jnp.bfloat16)
    value_grad = jnp.einsum(
        "rnhij,rnihd->rnjhd", scores_low, numer_grad, preferred_element_type=jnp.float32
    )
    query_grad = jnp.einsum(
        "rnhij,rnjhf->rnihf", score_grad, key_feats, preferred_element_type=jnp.float32
    )
    key_grad = jnp.einsum(
        "rnhij,rnihf->rnjhf", score_grad, query_feats, preferred_element_type=jnp.float32
    )
    masked_keys, prior_states, prior_sums = block_states(key_feats, values, in_last, linked)
    carried_grad = numer_grad * carried.astype(jnp.bfloat16)[..., None, None]
    den_carried = den_grad * carried[..., None]
    query_grad = query_grad + jnp.einsum(
        "rnihd,rnhfd->rnihf",
        carried_grad,
        prior_states.astype(jnp.bfloat16),
        preferred_element_type=jnp.float32,
    )
    query_grad = query_grad + den_carried[..., None] * prior_sums[:, :, None]
    prior_grad = jnp.einsum(
        "rnihf,rnihd->rnhfd", query_feats, carried_grad, preferred_element_type=jnp.float32
    )
    prior_sum_grad = jnp.einsum(
        "rnihf,rnih->rnhf", query_feats.astype(jnp.float32), den_carried, precision=highest
    )
    contrib_grad = jnp.einsum(
        "rcb,rchfd->rbhfd", linked, unshift_blocks(prior_grad), precision=highest
    ).astype(jnp.bfloat16)
    keysum_grad = jnp.einsum(
        "rcb,rchf->rbhf", linked, unshift_blocks(prior_sum_grad), precision=highest
    )
    masked_grad = (
        jnp.einsum("rnjhd,rnhfd->rnjhf", values, contrib_grad, preferred_element_type=jnp.float32)
        + keysum_grad[:, :, None]
    )
    key_grad = key_grad + jnp.where(in_last[..., None, None], masked_grad, 0.0)
    value_grad = value_grad + jnp.einsum(
        "rnjhf,rnhfd->rnjhd", masked_keys, contrib_grad, preferred_element_type=jnp.float32
    )
    return (query_grad, key_grad, value_grad)


def on_device(
    tokens,
    doc_starts,
    query_proj,
    key_proj,
    value_proj,
    query_bias,
    key_bias,
    value_bias,
    output_proj,
    output_bias,
    attn_gain,
    attn_shift,
    up_proj,
    up_bias,
    down_proj,
    down_bias,
    ffn_gain,
    ffn_shift,
    cotangent,
):
    batch_rows, shard_len, model_width = tokens.shape
    own_start = lax.axis_index("mp") * shard_len
    full_tokens = lax.all_gather(tokens, "mp", axis=1, tiled=True)
    full_len = full_tokens.shape[1]
    number, cos_part, sin_part = jax.vmap(doc_layout)(doc_starts)
    block_info = block_masks(number)
    weight_all = jnp.concatenate([query_proj, key_proj, value_proj], axis=1)
    bias_all = jnp.concatenate([query_bias, key_bias, value_bias])
    projected = rowwise(full_tokens, weight_all) + bias_all
    query_in = projected[..., :model_width]
    key_in = projected[..., model_width : 2 * model_width]
    value_in = projected[..., 2 * model_width :]
    query_feats = features(query_in, cos_part, sin_part)
    key_feats = features(key_in, cos_part, sin_part)
    values = value_in.astype(jnp.bfloat16).reshape(batch_rows, full_len // BLOCK, BLOCK, HEADS, HD)
    context, numerator, raw_den = attend(query_feats, key_feats, values, block_info)
    context_low = context.astype(jnp.bfloat16).reshape(batch_rows, full_len, model_width)
    own_context = lax.dynamic_slice_in_dim(context_low, own_start, shard_len, 1)
    hidden = tokens.astype(jnp.float32) + rowwise(own_context, output_proj) + output_bias
    normed, attn_pull = jax.vjp(layer_norm, hidden, attn_gain, attn_shift)
    full_normed = lax.all_gather(normed.astype(jnp.bfloat16), "mp", axis=1, tiled=True)
    upper = rowwise(full_normed, up_proj) + up_bias
    acted, gelu_pull = jax.vjp(partial(jax.nn.gelu, approximate=True), upper)
    acted_low = acted.astype(jnp.bfloat16)
    piece = lax.slice_in_dim(acted_low, 0, lax.axis_size("mp") * shard_len, axis=1)
    ffn_out = (
        lax.psum_scatter(
            jnp.einsum("rlf,fd->lrd", piece, down_proj, preferred_element_type=jnp.float32).astype(
                jnp.bfloat16
            ),
            "mp",
            scatter_dimension=0,
            tiled=True,
        )
        .astype(jnp.float32)
        .transpose(1, 0, 2)
    )
    merged = normed + ffn_out + down_bias
    result, final_pull = jax.vjp(layer_norm, merged, ffn_gain, ffn_shift)
    layer_out = result.astype(jnp.bfloat16)
    merged_grad, ffn_gain_grad, ffn_shift_grad = final_pull(cotangent.astype(jnp.float32))
    down_bias_grad = jnp.sum(merged_grad, axis=(0, 1))
    full_merged = lax.all_gather(merged_grad.astype(jnp.bfloat16), "mp", axis=1, tiled=True)
    down_proj_grad = jnp.einsum(
        "rlf,rld->fd", acted_low, full_merged, preferred_element_type=jnp.float32
    )
    acted_grad = jnp.einsum(
        "rld,fd->rlf", full_merged, down_proj, preferred_element_type=jnp.float32
    )
    (upper_grad,) = gelu_pull(acted_grad)
    up_bias_grad = jnp.sum(upper_grad, axis=(0, 1))
    upper_low = upper_grad.astype(jnp.bfloat16)
    up_proj_grad = jnp.einsum(
        "rld,rlf->df", full_normed, upper_low, preferred_element_type=jnp.float32
    )
    piece = upper_low
    normed_grad = (
        lax.psum_scatter(
            jnp.einsum("rlf,df->lrd", piece, up_proj, preferred_element_type=jnp.float32).astype(
                jnp.bfloat16
            ),
            "mp",
            scatter_dimension=0,
            tiled=True,
        )
        .astype(jnp.float32)
        .transpose(1, 0, 2)
        + merged_grad
    )
    hidden_grad, attn_gain_grad, attn_shift_grad = attn_pull(normed_grad)
    output_bias_grad = jnp.sum(hidden_grad, axis=(0, 1))
    hidden_low = hidden_grad.astype(jnp.bfloat16)
    output_proj_grad = jnp.einsum(
        "rld,rle->de", own_context, hidden_low, preferred_element_type=jnp.float32
    )
    own_context_grad = jnp.einsum(
        "rle,de->rld", hidden_low, output_proj, preferred_element_type=jnp.float32
    ).astype(jnp.bfloat16)
    context_grad = lax.all_gather(own_context_grad, "mp", axis=1, tiled=True)
    context_grad = context_grad.reshape(batch_rows, full_len // BLOCK, BLOCK, HEADS, HD)
    query_feat_grad, key_feat_grad, value_grad = attend_back(
        query_feats, key_feats, values, block_info, numerator, raw_den, context_grad
    )
    query_grad = features_back(query_in, cos_part, sin_part, query_feat_grad)
    key_grad = features_back(key_in, cos_part, sin_part, key_feat_grad)
    value_grad = value_grad.reshape(batch_rows, full_len, model_width)
    projected_grad = jnp.concatenate([query_grad, key_grad, value_grad], axis=2)
    projected_low = projected_grad.astype(jnp.bfloat16)
    own_grad = lax.dynamic_slice_in_dim(projected_low, own_start, shard_len, 1)
    input_grad = (
        jnp.einsum("rln,kn->rlk", own_grad, weight_all, preferred_element_type=jnp.float32)
        + hidden_grad
    ).astype(jnp.bfloat16)
    proj_grads = jnp.einsum(
        "rld,rlsc->sdc",
        tokens,
        own_grad.reshape(batch_rows, shard_len, 3, model_width),
        preferred_element_type=jnp.float32,
    )
    own_full = lax.dynamic_slice_in_dim(projected_grad, own_start, shard_len, 1)
    proj_bias = jnp.sum(own_full.reshape(batch_rows, shard_len, 3, model_width), axis=(0, 1))[
        :, None, :
    ]
    (
        proj_grads,
        proj_bias,
        output_proj_grad,
        output_bias_grad,
        attn_gain_grad,
        attn_shift_grad,
        down_bias_grad,
        ffn_gain_grad,
        ffn_shift_grad,
    ) = lax.psum(
        (
            proj_grads,
            proj_bias,
            output_proj_grad,
            output_bias_grad,
            attn_gain_grad,
            attn_shift_grad,
            down_bias_grad,
            ffn_gain_grad,
            ffn_shift_grad,
        ),
        ("dp", "mp"),
    )
    up_proj_grad, up_bias_grad, down_proj_grad = lax.psum(
        (up_proj_grad, up_bias_grad, down_proj_grad), "dp"
    )
    return (
        layer_out,
        input_grad,
        proj_grads[0],
        proj_grads[1],
        proj_grads[2],
        proj_bias[0, 0],
        proj_bias[1, 0],
        proj_bias[2, 0],
        output_proj_grad,
        output_bias_grad,
        attn_gain_grad,
        attn_shift_grad,
        up_proj_grad,
        up_bias_grad,
        down_proj_grad,
        down_bias_grad,
        ffn_gain_grad,
        ffn_shift_grad,
    )


def solution(mesh):
    placed = (
        P("dp", "mp", None),
        P("dp", None),
        P(),
        P(),
        P(),
        P(),
        P(),
        P(),
        P(),
        P(),
        P(),
        P(),
        P(None, "mp"),
        P("mp"),
        P("mp", None),
        P(),
        P(),
        P(),
        P("dp", "mp", None),
    )
    return jax.shard_map(
        on_device,
        mesh=mesh,
        in_specs=placed,
        out_specs=(
            P("dp", "mp", None),
            P("dp", "mp", None),
            P(),
            P(),
            P(),
            P(),
            P(),
            P(),
            P(),
            P(),
            P(),
            P(),
            P(None, "mp"),
            P("mp"),
            P("mp", None),
            P(),
            P(),
            P(),
        ),
        check_vma=False,
    )
```

profile of v0, /device:TPU:0, one launch (start us, length us, event | category | flops | bytes accessed | tf_op | source)
XLA Modules:
  0.0 802.0 jit_solution(18180714674823092605)
XLA Ops:
  20.9 28.6 %all-gather.6.cloned.1.call-done = bf16[1,1024,768]{2,1,0:T(8,128)(2,1)} async-done(((bf16[1,256,768]{2,1,0:T(8,128)(2,1)}), bf16[1,1024,768]{2,1,0:T(8,128)(2,1)}) %all-gather.6.cloned.1.call-update) | async-done | bytes 1572880 | tf_op jit(solution)/shard_map/all_gather | solution.py:218
  49.5 7.8 add_bitcast_fusion
  57.3 3.9 slice_maximum_fusion
  63.0 5.9 reshape.1061
  68.9 6.6 copy.180
  75.5 5.7 reshape.1062
  81.2 6.6 copy.182
  87.7 3.4 reshape.1060
  91.1 5.0 copy.196
  96.1 5.9 multiply_convert_fusion.3
  102.0 3.5 pad_maximum_fusion.1
  109.8 3.8 fusion.70
  114.9 2.7 convert_reduce_fusion
  118.6 5.0 fusion.92
  123.6 5.8 convert_bitcast_fusion
  130.7 7.2 fusion.5
  137.8 4.2 copy.192
  142.0 5.9 reshape.1065
  150.9 36.0 %all-gather.8.cloned.1.call-done = bf16[1,1024,768]{2,1,0:T(8,128)(2,1)} async-done(((bf16[1,256,768]{2,1,0:T(8,128)(2,1)}), bf16[1,1024,768]{2,1,0:T(8,128)(2,1)}) %all-gather.8.cloned.1.call-update) | async-done | bytes 1572880 | tf_op jit(solution)/shard_map/all_gather | solution.py:236
  186.9 3.1 fusion.58
  191.7 3.3 fusion.63
  195.0 34.2 %reduce-scatter.3.cloned.1.call-done = bf16[256,1,768]{2,0,1:T(8,128)(2,1)} async-done(((bf16[1024,1,768]{2,0,1:T(8,128)(2,1)}), bf16[256,1,768]{2,0,1:T(8,128)(2,1)}) %reduce-scatter.3.cloned.1.call-update) | async-done | bytes 393232 | tf_op jit(solution)/shard_map/reduce_scatter | solution.py:242
  234.6 36.2 %all-gather.10.cloned.1.call-done = bf16[1,1024,768]{2,1,0:T(8,128)(2,1)} async-done(((bf16[1,256,768]{2,1,0:T(8,128)(2,1)}), bf16[1,1024,768]{2,1,0:T(8,128)(2,1)}) %all-gather.10.cloned.1.call-update) | async-done | bytes 1572880 | tf_op jit(solution)/shard_map/all_gather | solution.py:258
  270.8 6.3 fusion.129
  278.2 2.6 fusion.64
  280.9 34.3 %reduce-scatter.5.cloned.1.call-done = bf16[256,1,768]{2,0,1:T(8,128)(2,1)} async-done(((bf16[1024,1,768]{2,0,1:T(8,128)(2,1)}), bf16[256,1,768]{2,0,1:T(8,128)(2,1)}) %reduce-scatter.5.cloned.1.call-update) | async-done | bytes 393232 | tf_op jit(solution)/shard_map/reduce_scatter | solution.py:273
  322.2 3.0 fusion.81
  325.1 32.4 %all-gather.12.cloned.1.call-done = bf16[1024,768]{1,0:T(8,128)(2,1)} async-done(((bf16[256,768]{1,0:T(8,128)(2,1)}), bf16[1024,768]{1,0:T(8,128)(2,1)}) %all-gather.12.cloned.1.call-update) | async-done | bytes 1572880 | tf_op jit(solution)/shard_map/all_gather | solution.py:294
  357.6 3.2 copy.193
  360.8 5.7 reshape.1081
  366.5 5.7 broadcast_multiply_fusion
  372.2 4.6 fusion.36
  376.8 5.5 fusion.26
  382.3 4.5 reshape.1097
  386.8 8.7 %copy.198 = f32[1,16,64,12,64]{2,4,3,1,0:T(8,128)} copy(f32[1,16,64,12,64]{4,3,2,1,0:T(8,128)} %reshape.1097) | data formatting | bytes 6291456 | tf_op jit(solution)/shard_map/convert_element_type | solution.py:140
  395.5 6.7 fusion.6
  402.4 2.6 fusion.90
  409.0 3.3 slice.92
  412.3 3.4 pad_bitcast_fusion
  415.8 6.0 fusion.47
  421.9 4.6 fusion.22
  426.5 2.6 fusion.4
  430.2 7.4 bitcast_add_fusion
  437.6 3.4 copy.204
  441.0 6.4 fusion.1
  447.4 6.1 copy.205
  453.5 6.3 copy.212
  459.8 6.9 add_bitcast_fusion.1
  466.7 7.0 copy.216
  473.7 6.3 concatenate.92
  480.0 9.5 %bitcast_select_fusion.1 = (f32[1,1024,768]{1,2,0:T(8,128)}, f32[1,1024,768]{1,2,0:T(8,128)}) fusion(f32[1,1024,12,64]{1,3,2,0:T(8,128)} %copy.205, f32[1,1024,2304]{1,2,0:T(8,128)} %copy-done.9, f32[1,1024,12,64]{1,3,2,0:T(8,128)} %copy.212), kind=kLoop, calls=%fused_computation.47 | loop fusion | flops 3145728 | bytes 18874368 | tf_op jit(solution)/shard_map/jit(_where)/select_n | solution.py:61
  489.5 9.4 %pad_maximum_fusion = f32[1,1024,2304]{1,2,0:T(8,128)} fusion(f32[1,1024,768]{1,2,0:T(8,128)} %concatenate.92, f32[1,1024,768]{1,2,0:T(8,128)} %get-tuple-element.144, f32[1,1024,768]{1,2,0:T(8,128)} %get-tuple-element.143), kind=kLoop, calls=%fused_computation | loop fusion | flops 4718592 | bytes 18874368 | tf_op jit(solution)/shard_map/concatenate | solution.py:302
  500.6 4.0 convolution_bitcast_fusion
  504.9 5.0 fusion.56
  510.0 3.4 fusion.50
  514.0 14.3 %psum.91 = f32[768]{0:T(1024)} all-reduce(f32[768]{0:T(1024)S(1)} %copy-done.60), channel_id=1, replica_groups=mesh['dp'=8,'mp'=4] {'dp'}, use_global_device_ids=true, to_apply=%region_28.29 | all-reduce | flops 768 | bytes 6144 | tf_op jit(solution)/shard_map/psum | solution.py:343
  530.7 40.4 %all-reduce.4 = (f32[3,1,768]{2,1,0:T(1,128)S(1)}, f32[768]{0:T(1024)}, f32[768]{0:T(1024)}, f32[768]{0:T(1024)}, f32[768]{0:T(1024)}, /*index=5*/f32[768]{0:T(1024)}, f32[768]{0:T(1024)}) all-reduce(f32[3,1,768]{2,1,0:T(1,128)S(1)} %broadcast_in_dim.153, f32[768]{0:T(1024)S(1)} %add_reduce_fusion, ...), channel_id=1, replica_groups=mesh['dp'=8,'mp'=4] {'dp','mp'}, use_global_device_ids=true, to_apply=%region_18.19 | all-reduce | flops 6912 | bytes 55296 | tf_op jit(solution)/shard_map/psum | solution.py:329
  571.7 3.9 fusion.68
  575.6 120.7 %all-reduce.10.cloned.1.call-done = (f32[3,768,768]{1,2,0:T(8,128)}, f32[768,768]{1,0:T(8,128)}) async-done(((f32[3,768,768]{1,2,0:T(8,128)}, f32[768,768]{1,0:T(8,128)}), (f32[3,768,768]{1,2,0:T(8,128)}, f32[768,768]{1,0:T(8,128)})) %all-reduce.10.cloned.1.call-update) | async-done | bytes 9437200 | tf_op jit(solution)/shard_map/psum | solution.py:329
  696.3 5.7 slice_bitcast_fusion
  702.0 3.0 copy.217
  705.0 3.7 copy.218
  710.6 77.0 %all-reduce.12.cloned.1.call-done = (f32[768,768]{1,0:T(8,128)}, f32[768,768]{1,0:T(8,128)}) async-done(((f32[768,768]{1,0:T(8,128)}, f32[768,768]{1,0:T(8,128)}), (f32[768,768]{1,0:T(8,128)}, f32[768,768]{1,0:T(8,128)})) %all-reduce.12.cloned.1.call-update) | async-done | bytes 4718608 | tf_op jit(solution)/shard_map/psum | solution.py:343
  787.6 3.4 copy.291
  (222 shorter events, 57.9 us)
Async XLA Ops:
  7.2 184.5 %copy-start = (bf16[768,768]{1,0:T(8,128)(2,1)S(1)}, bf16[768,768]{1,0:T(8,128)(2,1)}, u32[]{:S(2)}) copy-start(bf16[768,768]{1,0:T(8,128)(2,1)} %param.33) | copy-start | bytes 3538948
  7.2 11.4 %copy-start.22 = (bf16[768,768]{1,0:T(8,128)(2,1)S(1)}, bf16[768,768]{1,0:T(8,128)(2,1)}, u32[]{:S(2)}) copy-start(bf16[768,768]{1,0:T(8,128)(2,1)} %param.22) | copy-start | bytes 3538948
  7.2 11.5 %copy-start.23 = (bf16[768,768]{1,0:T(8,128)(2,1)S(1)}, bf16[768,768]{1,0:T(8,128)(2,1)}, u32[]{:S(2)}) copy-start(bf16[768,768]{1,0:T(8,128)(2,1)} %param.23) | copy-start | bytes 3538948
  7.2 42.2 %all-gather.6.cloned.1.call-start = ((), (), s32[]{:S(2)}) async-start(), calls=%async_computation.2 | async-start | bytes 1966080 | tf_op jit(solution)/shard_map/all_gather | solution.py:218
  8.0 178.9 %all-gather.8.cloned.1.call-start = ((), (), s32[]{:S(2)}) async-start(), calls=%async_computation.3 | async-start | bytes 1966080 | tf_op jit(solution)/shard_map/all_gather | solution.py:236
  12.9 5.8 copy-start.39
  17.2 3.4 copy-start.43
  20.6 94.3 %copy-start.35 = (pred[16,64]{1,0:T(8,128)(4,1)}, pred[16,64]{1,0:T(8,128)(4,1)S(1)}, u32[]{:S(2)}) copy-start(pred[16,64]{1,0:T(8,128)(4,1)S(1)} %get-tuple-element.165) | copy-start | bytes 3076
  20.9 86.5 %copy-start.20 = (pred[16,64,64]{1,2,0:T(8,128)(4,1)}, pred[16,64,64]{1,2,0:T(8,128)(4,1)S(1)}, u32[]{:S(2)}) copy-start(pred[16,64,64]{1,2,0:T(8,128)(4,1)S(1)} %compare_and_fusion) | copy-start | bytes 196612
  57.3 5.5 copy-start.9
  105.5 8.0 copy-start.4
  105.6 25.1 %copy-start.6 = (bf16[16,64,12,128]{3,1,2,0:T(8,128)(2,1)}, bf16[16,64,12,128]{3,1,2,0:T(8,128)(2,1)S(1)}, u32[]{:S(2)}) copy-start(bf16[16,64,12,128]{3,1,2,0:T(8,128)(2,1)S(1)} %get-tuple-element.174) | copy-start | bytes 9437188
  105.6 4.2 copy-start.2
  107.4 6.2 copy-start.10
  107.4 23.2 %copy-start.24 = (f32[16,12,64]{2,1,0:T(8,128)}, f32[16,12,64]{2,1,0:T(8,128)S(1)}, u32[]{:S(2)}) copy-start(f32[16,12,64]{2,1,0:T(8,128)S(1)} %get-tuple-element.166) | copy-start | bytes 147460
  123.6 7.1 copy-start.28
  130.6 7.2 copy-start.12
  130.7 7.2 copy-start.26
  142.0 5.9 copy-start.15
  142.0 5.9 copy-start.16
  142.0 7.8 copy-start.32
  149.5 79.8 %copy-start.37 = (f32[256]{0:T(256)}, f32[256]{0:T(256)S(1)}, u32[]{:S(2)}) copy-start(f32[256]{0:T(256)S(1)} %broadcast_multiply_fusion.2) | copy-start | bytes 3076
  149.8 37.1 %copy-start.57 = (f32[256]{0:T(256)}, f32[256]{0:T(256)S(1)}, u32[]{:S(2)}) copy-start(f32[256]{0:T(256)S(1)} %multiply_reduce_fusion.3) | copy-start | bytes 3076
  149.8 79.5 %copy-start.44 = (f32[256]{0:T(256)}, f32[256]{0:T(256)S(1)}, u32[]{:S(2)}) copy-start(f32[256]{0:T(256)S(1)} %fusion.106) | copy-start | bytes 3076
  150.8 40.9 %copy-start.63 = (f32[768]{0:T(1024)S(1)}, f32[768]{0:T(1024)}, u32[]{:S(2)}) copy-start(f32[768]{0:T(1024)} %param.32) | copy-start | bytes 9220
  150.8 78.5 %reduce-scatter.3.cloned.1.call-start = ((), (), s32[]{:S(2)}) async-start(), calls=%async_computation.4 | async-start | bytes 1966080 | tf_op jit(solution)/shard_map/reduce_scatter | solution.py:242
  191.7 37.6 %copy-start.47 = (f32[768]{0:T(1024)S(1)}, f32[768]{0:T(1024)}, u32[]{:S(2)}) copy-start(f32[768]{0:T(1024)} %param.30) | copy-start | bytes 9220
  191.7 37.6 %copy-start.59 = (f32[768]{0:T(1024)S(1)}, f32[768]{0:T(1024)}, u32[]{:S(2)}) copy-start(f32[768]{0:T(1024)} %param.34) | copy-start | bytes 9220
  195.0 36.0 %copy-start.19 = (bf16[1,256,768]{2,1,0:T(8,128)(2,1)S(1)}, bf16[1,256,768]{2,1,0:T(8,128)(2,1)}, u32[]{:S(2)}) copy-start(bf16[1,256,768]{2,1,0:T(8,128)(2,1)} %param.37) | copy-start | bytes 1179652
  195.0 36.0 %copy-start.48 = (f32[768]{0:T(1024)S(1)}, f32[768]{0:T(1024)}, u32[]{:S(2)}) copy-start(f32[768]{0:T(1024)} %param.35) | copy-start | bytes 9220
  195.0 75.8 %all-gather.10.cloned.1.call-start = ((), (), s32[]{:S(2)}) async-start(), calls=%async_computation.5 | async-start | bytes 1966080 | tf_op jit(solution)/shard_map/all_gather | solution.py:258
  234.6 80.6 %reduce-scatter.5.cloned.1.call-start = ((), (), s32[]{:S(2)}) async-start(), calls=%async_computation.6 | async-start | bytes 1966080 | tf_op jit(solution)/shard_map/reduce_scatter | solution.py:273
  270.8 7.4 copy-start.62
  278.2 36.9 %copy-start.38 = (f32[256]{0:T(256)S(1)}, f32[256]{0:T(256)}, u32[]{:S(2)}) copy-start(f32[256]{0:T(256)} %copy-done.37) | copy-start | bytes 3076
  278.2 36.9 %copy-start.45 = (f32[256]{0:T(256)S(1)}, f32[256]{0:T(256)}, u32[]{:S(2)}) copy-start(f32[256]{0:T(256)} %copy-done.44) | copy-start | bytes 3076
  280.8 36.4 %copy-start.58 = (f32[256]{0:T(256)S(1)}, f32[256]{0:T(256)}, u32[]{:S(2)}) copy-start(f32[256]{0:T(256)} %copy-done.57) | copy-start | bytes 3076
  280.8 76.7 %all-gather.12.cloned.1.call-start = ((), (), s32[]{:S(2)}) async-start(), calls=%async_computation.7 | async-start | bytes 1966080 | tf_op jit(solution)/shard_map/all_gather | solution.py:294
  317.3 4.2 copy-start.40
  317.3 4.2 copy-start.41
  317.3 4.8 copy-start.27
  317.3 4.9 copy-start.30
  321.4 374.9 %all-reduce.10.cloned.1.call-start = ((), (), s32[]{:S(2)}) async-start(), calls=%async_computation.8 | async-start | bytes 18874368 | tf_op jit(solution)/shard_map/psum | solution.py:329
  360.8 5.7 copy-start.54
  366.5 5.7 copy-start.7
  372.2 4.6 copy-start.13
  376.8 5.5 copy-start.14
  395.5 6.8 copy-start.25
  395.5 6.8 copy-start.29
  395.5 6.9 copy-start.8
  395.5 9.8 %copy-start.11 = (bf16[16,64,12,64]{1,0,3,2:T(8,128)(2,1)S(1)}, bf16[16,64,12,64]{1,0,3,2:T(8,128)(2,1)}, u32[]{:S(2)}) copy-start(bf16[16,64,12,64]{1,0,3,2:T(8,128)(2,1)} %get-tuple-element.134) | copy-start | bytes 4718596
  415.8 6.1 copy-start.5
  415.8 6.1 copy-start.36
  437.6 3.4 copy-start.55
  437.6 3.4 copy-start.56
  504.6 5.3 copy-start.64
  504.6 283.0 %all-reduce.12.cloned.1.call-start = ((), (), s32[]{:S(2)}) async-start(), calls=%async_computation.9 | async-start | bytes 9437184 | tf_op jit(solution)/shard_map/psum | solution.py:343
  504.9 5.1 copy-start.61
  504.9 5.1 copy-start.66
  513.3 17.3 %copy-start.49 = (f32[768]{0:T(1024)S(1)}, f32[768]{0:T(1024)}, u32[]{:S(2)}) copy-start(f32[768]{0:T(1024)} %get-tuple-element.110) | copy-start | bytes 9220
  513.3 17.3 %copy-start.50 = (f32[768]{0:T(1024)S(1)}, f32[768]{0:T(1024)}, u32[]{:S(2)}) copy-start(f32[768]{0:T(1024)} %get-tuple-element.114) | copy-start | bytes 9220
  513.4 17.3 %copy-start.51 = (f32[768]{0:T(1024)S(1)}, f32[768]{0:T(1024)}, u32[]{:S(2)}) copy-start(f32[768]{0:T(1024)} %get-tuple-element.108) | copy-start | bytes 9220
  513.4 17.3 %copy-start.52 = (f32[768]{0:T(1024)S(1)}, f32[768]{0:T(1024)}, u32[]{:S(2)}) copy-start(f32[768]{0:T(1024)} %get-tuple-element.112) | copy-start | bytes 9220
  513.4 17.3 %copy-start.53 = (f32[768]{0:T(1024)S(1)}, f32[768]{0:T(1024)}, u32[]{:S(2)}) copy-start(f32[768]{0:T(1024)} %get-tuple-element.113) | copy-start | bytes 9220
  791.0 3.9 copy-start.1
  (14 other events, 32.8 us)
Sparse Core Ops, SparseCore 0:
  9.6 39.7 all-gather.5
  150.9 35.9 all-gather.7
  195.1 34.1 reduce-scatter.2
  234.7 36.0 all-gather.9
  281.0 34.1 reduce-scatter.4
  321.5 36.0 all-gather.11
  504.8 191.4 all-reduce.9
  700.6 87.0 all-reduce.11
where the time goes:
time: 809 us; the launch traced here: 802 us
  waiting for transfers between devices  400 us (49%)
  local copies, waits for them, and re-layouts  144 us (18%)
  matrix products  115 us (14%)
  other arithmetic  71.9 us (9%)
  blocking collectives  54.7 us (7%)
  between operations  15.3 us (2%)
    psum x1, waiting for transfers between devices, on_device(): lax.psum((proj_grads, proj_bias, output_proj_grad, output_bias_grad, attn...  121 us
    psum x1, waiting for transfers between devices, on_device(): lax.psum((up_proj_grad, up_bias_grad, down_proj_grad), 'dp')  77 us
    psum x1, blocking collectives, on_device(): lax.psum((proj_grads, proj_bias, output_proj_grad, output_bias_grad, attn...  40.4 us
    all_gather x1, waiting for transfers between devices, on_device(): lax.all_gather(merged_grad.astype(jnp.bfloat16), 'mp', axis=1, tiled=True)  36.2 us
    all_gather x1, waiting for transfers between devices, on_device(): lax.all_gather(normed.astype(jnp.bfloat16), 'mp', axis=1, tiled=True)  36 us
    reduce_scatter x1, waiting for transfers between devices, on_device(): lax.psum_scatter(jnp.einsum('rlf,df->lrd', piece, up_proj, preferred_elem...  34.3 us
    reduce_scatter x1, waiting for transfers between devices, on_device(): lax.psum_scatter(jnp.einsum('rlf,fd->lrd', piece, down_proj, preferred_el...  34.2 us
    all_gather x1, waiting for transfers between devices, on_device(): context_grad = lax.all_gather(own_context_grad, 'mp', axis=1, tiled=True)  32.4 us
  transfers between devices with their start and end apart: 8, of which 8 were waited for; matrix products, arithmetic and copies ran while one was open for 6% of the time, Pallas kernels for 0%

commit v1 on v0

v1 whole, which is shorter than its diff:
```python
import math

import jax
import jax.numpy as jnp
from jax import lax
from jax.experimental import pallas as pl
from jax.experimental.pallas import tpu as pltpu
from jax.sharding import PartitionSpec as P

HEADS = 12
HD = 64
SEQ = 1024
DOCS = 2
PAIR = 2 * HD
PAIRS = HEADS // 2
TILE = 256
MESH = pl.DeviceIdType.MESH
BF = jnp.bfloat16
F32 = jnp.float32
C0 = math.sqrt(2.0 / math.pi)
C1 = 0.044715


def mm(a, b):
    return lax.dot_general(a, b, (((1,), (0,)), ((), ())), preferred_element_type=F32)


def mm_nt(a, b):
    return lax.dot_general(a, b, (((1,), (1,)), ((), ())), preferred_element_type=F32)


def mm_tn(a, b):
    return lax.dot_general(a, b, (((0,), (0,)), ((), ())), preferred_element_type=F32)


def gelu_both(u):
    square = u * u
    t = jnp.tanh(C0 * u * (1.0 + C1 * square))
    half = 0.5 * (1.0 + t)
    slope = half + (0.5 * C0) * u * (1.0 - t * t) * (1.0 + (3.0 * C1) * square)
    return u * half, slope


def two_parts(x):
    high = x.astype(BF)
    return jnp.concatenate([high, (x - high.astype(F32)).astype(BF)], axis=1)


def col_sum(x):
    return jnp.sum(x, axis=0, keepdims=True)


def build(dp_size, mp_size, rows, width, shard):
    nbits = dp_size.bit_length() - 1
    nhalf = min(3, nbits)
    slices = 1 << nhalf
    piece = width >> nhalf
    ALL = pl.ds(0, rows)

    def order(kind):
        first = list(range(nhalf))
        if kind == 1 and nhalf == 3:
            first = [0, 2, 1]
        return first

    def w_order(kind):
        plain = order(kind)
        return plain[1:] + plain[:1]

    jobs = [order(0), order(1), order(0), order(1), order(0), order(1)]

    def kernel(
        starts, tok, cot, wq, wk, wv, wo, vec, up_hbm, down_hbm,
        out_layer, out_input, out_attn, out_ff, out_small,
        wu, wd, ub, rq, rk, vv, m2, mt2, cols, o2, bb, c1, ec, masks,
        state, state_in, ssum, ssum_in, grad_in, gsum_in, state_out, ssum_out, grad_out, gsum_out,
        num, den, ctx, hid, rstd, normed, nf, mf, acted, gps, acc, mg, ulow, hlow, cg, ngr, dgr,
        gq, gk, gv, part, gsum, red0, red1, red2, redx, zr, small, smallr, smallz, tokt, in_out,
        local_sem, send_sem, recv_sem,
    ):
        dp = lax.axis_index("dp")
        mp = lax.axis_index("mp")
        counter = [0]
        locals_used = [0]

        def bit(b):
            return lax.rem(lax.div(dp, 1 << b), 2)

        def flip(b):
            return {"dp": dp + (1 - 2 * bit(b)) * (1 << b)}

        def peer(r):
            return {"mp": lax.rem(mp + r, mp_size)}

        def remote(src, dst, device):
            i = counter[0]
            counter[0] += 1
            return pltpu.make_async_remote_copy(
                src_ref=src, dst_ref=dst, send_sem=send_sem.at[i], recv_sem=recv_sem.at[i],
                device_id=device, device_id_type=MESH,
            )

        def local(src, dst):
            i = locals_used[0]
            locals_used[0] += 1
            return pltpu.make_async_copy(src, dst, local_sem.at[i])

        def rds(start, size, unit=16):
            return pl.ds(pl.multiple_of(start, unit), size)

        barrier = pltpu.get_barrier_semaphore()
        for b in range(nbits):
            pl.semaphore_signal(barrier, inc=1, device_id=flip(b), device_id_type=MESH)
        for r in range(1, mp_size):
            pl.semaphore_signal(barrier, inc=1, device_id=peer(r), device_id_type=MESH)
        own_up = local(up_hbm, wu.at[mp])
        own_down = local(down_hbm, wd.at[mp])
        own_up.start()
        own_down.start()
        ub[mp] = jnp.broadcast_to(vec[15:16, :], (8, shard))
        own_up.wait()
        own_down.wait()
        pl.semaphore_wait(barrier, nbits + mp_size - 1)

        def w_base(kind, upto):
            bits = w_order(kind)
            base = 0
            for s in range(nhalf - 1, upto - 1, -1):
                base = base + bit(bits[s]) * (piece << s)
            return base

        w_stages = []
        stage = []
        for kind, buf in ((0, wu), (1, wd)):
            base = w_base(kind, 0)
            for r in range(1, mp_size):
                ref = buf.at[mp, rds(base, piece)]
                stage.append(remote(ref, ref, peer(r)))
        for r in range(1, mp_size):
            stage.append(remote(ub.at[mp], ub.at[mp], peer(r)))
        w_stages.append(stage)
        for s in range(nhalf):
            stage = []
            for kind, buf in ((0, wu), (1, wd)):
                base = w_base(kind, s)
                for r in range(1, mp_size):
                    t = lax.rem(mp + r, mp_size)
                    ref = buf.at[t, rds(base, piece << s)]
                    stage.append(remote(ref, ref, flip(w_order(kind)[s])))
            w_stages.append(stage)

        def weights_step(s):
            if s > 0:
                for copy in w_stages[s - 1]:
                    copy.wait()
            if s < len(w_stages):
                for copy in w_stages[s]:
                    copy.start()

        weights_step(0)

        own_start = mp * rows

        def layout(places):
            opened = jnp.full(places.shape, 0, jnp.int32) + starts[0, 0]
            closed = jnp.full(places.shape, SEQ, jnp.int32)
            if DOCS > 1:
                closed = jnp.full(places.shape, 0, jnp.int32) + starts[0, 1]
            number = jnp.zeros(places.shape, jnp.int32)
            for d in range(1, DOCS):
                ending = starts[0, d + 1] if d + 1 < DOCS else SEQ
                inside = places >= starts[0, d]
                opened = jnp.where(inside, starts[0, d], opened)
                closed = jnp.where(inside, ending, closed)
                number = number + inside.astype(jnp.int32)
            angles = (places - opened).astype(F32) * (0.5 * math.pi) / (closed - opened).astype(F32)
            return number, jnp.cos(angles), jnp.sin(angles)

        places = own_start + lax.broadcasted_iota(jnp.int32, (rows, 128), 0)
        number_c, cos_c, sin_c = layout(places)
        row_places = own_start + lax.broadcasted_iota(jnp.int32, (8, rows), 1)
        number_r, cos_r, sin_r = layout(row_places)
        edge = jnp.zeros((8, 128), jnp.int32)
        last, _, _ = layout(edge + own_start + (rows - 1))
        before, _, _ = layout(edge + own_start - 1)
        has_prev = jnp.where(edge + mp > 0, 1.0, 0.0)
        carried = jnp.where(number_c == before[:1], 1.0, 0.0) * has_prev[:1]
        in_last = jnp.where(number_c == last[:1], 1.0, 0.0)
        linked = (jnp.where(before == last, 1.0, 0.0) * has_prev)[:1]
        cols[0] = cos_c * carried
        cols[1] = sin_c * carried
        cols[2] = cos_c * in_last
        cols[3] = sin_c * in_last
        linked2 = jnp.concatenate([linked, linked], axis=1)
        linked6 = jnp.concatenate([linked] * (width // 128), axis=1)
        wide = jnp.concatenate([number_c, number_c], axis=1)
        wide_cos = jnp.concatenate([cos_c, cos_c], axis=1)
        wide_sin = jnp.concatenate([sin_c, sin_c], axis=1)
        row_id = lax.broadcasted_iota(jnp.int32, (rows, rows), 0)
        col_id = lax.broadcasted_iota(jnp.int32, (rows, rows), 1)
        angle_gap = wide_cos * cos_r[:1] + wide_sin * sin_r[:1]
        same = wide == number_r[:1]
        lower = jnp.where(same & (col_id <= row_id), angle_gap, 0.0)
        upper_part = jnp.where(same & (col_id >= row_id), angle_gap, 0.0)
        m2[:, :rows] = lower
        m2[:, rows:] = lower
        mt2[:, :rows] = upper_part
        mt2[:, rows:] = upper_part

        lane = lax.broadcasted_iota(jnp.int32, (rows, PAIR), 1)
        low_f = jnp.where(lane < HD, 1.0, 0.0)
        high_f = 1.0 - low_f
        first_two = jnp.where(lax.rem(lane, HD) < 2, 1.0, 0.0)
        o2[:rows, :] = low_f.astype(BF)
        o2[rows:, :] = high_f.astype(BF)
        c1[:rows, :] = (first_two * low_f).astype(BF)
        c1[rows:, :] = (first_two * high_f).astype(BF)
        ec[...] = first_two.astype(BF)
        block_row = lax.broadcasted_iota(jnp.int32, (2 * PAIR, PAIR), 0)
        block_col = lax.broadcasted_iota(jnp.int32, (2 * PAIR, PAIR), 1)
        bb[...] = jnp.where(
            lax.div(lax.rem(block_row, PAIR), HD) == lax.div(block_col, HD), 1.0, 0.0
        ).astype(BF)
        lo = low_f.astype(BF)[:16]
        hi = high_f.astype(BF)[:16]
        masks[0] = lo
        masks[1] = hi
        masks[2] = jnp.where(lax.rem(lane, HD) == 0, 1.0, 0.0).astype(BF)[:16]
        masks[3] = jnp.where(lax.rem(lane, HD) == 1, 1.0, 0.0).astype(BF)[:16]

        def halves(x):
            return jnp.concatenate([x * masks[0, :1], x * masks[1, :1]], axis=0)

        def expand(compact):
            low4 = jnp.concatenate([masks[0, :1]] * 2, axis=1)
            high4 = jnp.concatenate([masks[1, :1]] * 2, axis=1)
            return jnp.concatenate([compact * low4, compact * high4], axis=0)

        def compact_of(full):
            low4 = jnp.concatenate([masks[0, :1]] * 2, axis=1).astype(F32)
            high4 = jnp.concatenate([masks[1, :1]] * 2, axis=1).astype(F32)
            return full[:HD] * low4 + full[HD:] * high4

        for index, (weight, out) in enumerate(((wq, rq), (wk, rk), (wv, vv))):
            for j in range(width // TILE):
                at = pl.ds(j * TILE, TILE)
                y = mm(tok[...], weight[:, at]) + vec[index : index + 1, at]
                if index < 2:
                    y = jnp.maximum(y, 0.0)
                out[:, at] = y.astype(BF)

        def lanes(p):
            return pl.ds(pl.multiple_of(p * PAIR, PAIR), PAIR)

        def feats(ref, p, which):
            x = ref[:, lanes(p)].astype(F32)
            return (x * cols[which]).astype(BF), (x * cols[which + 1]).astype(BF)

        def contribs(p, carry):
            kc, ks = feats(rk, p, 2)
            full = mm_tn(vv[:, lanes(p)], jnp.concatenate([kc, ks], axis=1))
            state[p] = compact_of(full)
            ssum[0:1, lanes(p)] = col_sum(kc.astype(F32))
            ssum[1:2, lanes(p)] = col_sum(ks.astype(F32))
            return carry

        ssum[...] = jnp.zeros_like(ssum)
        lax.fori_loop(0, PAIRS, contribs, 0)

        def local_attention(p, carry):
            k2 = halves(rk[:, lanes(p)])
            a = (mm_nt(rq[:, lanes(p)], k2) * m2[...]).astype(BF)
            both = mm(a, jnp.concatenate([halves(vv[:, lanes(p)]), o2[...]], axis=1))
            num[:, lanes(p)] = both[:, :PAIR]
            den[:, lanes(p)] = both[:, PAIR:]
            return carry

        def chain(out_state, out_sum, in_state, in_sum, source, source_sum, forward):
            step = 1 if forward else mp_size - 1
            has_in = (mp > 0) if forward else (mp < mp_size - 1)
            has_out = (mp < mp_size - 1) if forward else (mp > 0)
            copies = [
                remote(out_state, in_state, peer(step)),
                remote(out_sum, in_sum, peer(step)),
            ]

            @pl.when(jnp.logical_not(has_in))
            def _():
                in_state[...] = jnp.zeros_like(in_state)
                in_sum[...] = jnp.zeros_like(in_sum)

            @pl.when(has_in)
            def _():
                for copy in copies:
                    copy.wait_recv()

            def fill(p, carry):
                value = source[p] + in_state[p].astype(F32) * linked2
                out_state[p] = value.astype(BF)
                return carry

            lax.fori_loop(0, PAIRS, fill, 0)
            out_sum[...] = source_sum[...] + in_sum[...] * linked6

            @pl.when(has_out)
            def _():
                for copy in copies:
                    copy.start()

            def finish():
                @pl.when(has_out)
                def _():
                    for copy in copies:
                        copy.wait_send()

            return finish

        lax.fori_loop(0, PAIRS, local_attention, 0)
        finish_forward = chain(state_out, ssum_out, state_in, ssum_in, state, ssum, True)
        weights_step(1)

        def remote_attention(p, carry):
            at = lanes(p)
            qc, qs = feats(rq, p, 0)
            carry_num = mm_nt(jnp.concatenate([qc, qs], axis=1), expand(state_in[p]))
            weighted = qc.astype(F32) * ssum_in[0:1, at] + qs.astype(F32) * ssum_in[1:2, at]
            total = den[:, at] + mm(two_parts(weighted), bb[...])
            value = (num[:, at] + carry_num) / jnp.maximum(total, 1.0)
            den[:, at] = total
            num[:, at] = value
            ctx[:, at] = value.astype(BF)
            return carry

        lax.fori_loop(0, PAIRS, remote_attention, 0)

        for j in range(width // TILE):
            at = pl.ds(j * TILE, TILE)
            hid[:, at] = tok[:, at].astype(F32) + mm(ctx[...], wo[:, at]) + vec[3:4, at]
        weights_step(2)
        RB = 64

        def first_norm(i, carry):
            at = pl.ds(pl.multiple_of(i * RB, RB), RB)
            x = hid[at, :]
            center = x - jnp.mean(x, axis=1, keepdims=True)
            inv = lax.rsqrt(jnp.mean(center * center, axis=1, keepdims=True) + 1e-05)
            xhat = center * inv
            y = xhat * vec[4:5, :] + vec[5:6, :]
            hid[at, :] = xhat
            rstd[at, :] = jnp.broadcast_to(inv, (RB, 128))
            normed[at, :] = y
            nf[mp, at, :] = y.astype(BF)
            return carry

        lax.fori_loop(0, rows // RB, first_norm, 0)
        norm_copies = [remote(nf.at[mp], nf.at[mp], peer(r)) for r in range(1, mp_size)]
        for copy in norm_copies:
            copy.start()
        weights_step(3)
        weights_step(4)

        def ffn_up(r, carry):
            t = lax.rem(mp + r, mp_size)
            for j in range(shard // TILE):
                at = pl.ds(j * TILE, TILE)
                u = mm(nf[mp], wu[t, :, at]) + ub[t, 0:1, at]
                value, slope = gelu_both(u)
                acted[t, :, at] = value.astype(BF)
                gps[t, :, at] = slope
            return carry

        lax.fori_loop(0, mp_size, ffn_up, 0)
        acc[...] = jnp.zeros_like(acc)

        def ffn_down(r, carry):
            t = lax.rem(mp + r, mp_size)
            for j in range(width // TILE):
                at = pl.ds(j * TILE, TILE)
                acc[:, at] += mm(acted[t], wd[t, :, at])
            return carry

        lax.fori_loop(0, mp_size, ffn_down, 0)
        small[0] = jnp.zeros_like(small[0])

        def second_norm(i, carry):
            at = pl.ds(pl.multiple_of(i * RB, RB), RB)
            x = normed[at, :] + acc[at, :] + vec[6:7, :]
            center = x - jnp.mean(x, axis=1, keepdims=True)
            inv = lax.rsqrt(jnp.mean(center * center, axis=1, keepdims=True) + 1e-05)
            xhat = center * inv
            in_out[0, at, :] = (xhat * vec[7:8, :] + vec[8:9, :]).astype(BF)
            g = cot[at, :].astype(F32)
            s = g * vec[7:8, :]
            grad = (
                s - jnp.mean(s, axis=1, keepdims=True) - xhat * jnp.mean(s * xhat, axis=1, keepdims=True)
            ) * inv
            mg[at, :] = grad
            mf[mp, at, :] = grad.astype(BF)
            small[0, 7:8, :] += col_sum(g * xhat)
            small[0, 8:9, :] += col_sum(g)
            small[0, 6:7, :] += col_sum(grad)
            return carry

        lax.fori_loop(0, rows // RB, second_norm, 0)
        layer_copy = local(in_out.at[0], out_layer)
        layer_copy.start()
        merged_copies = [remote(mf.at[mp], mf.at[mp], peer(r)) for r in range(1, mp_size)]
        for copy in merged_copies:
            copy.start()

        def ffn_back(r, carry):
            t = lax.rem(mp + r, mp_size)
            for j in range(shard // TILE):
                at = pl.ds(j * TILE, TILE)
                up_grad = mm_nt(mf[mp], wd[t, at, :]) * gps[t, :, at]
                ulow[:, at] = up_grad.astype(BF)
            for j in range(width // TILE):
                at = pl.ds(j * TILE, TILE)
                mg[:, at] += mm_nt(ulow[...], wu[t, at, :])
            return carry

        lax.fori_loop(0, mp_size, ffn_back, 0)

        def norm_back(i, carry):
            at = pl.ds(pl.multiple_of(i * RB, RB), RB)
            g = mg[at, :]
            xhat = hid[at, :]
            s = g * vec[4:5, :]
            inv = rstd[at, 0:1]
            grad = (
                s - jnp.mean(s, axis=1, keepdims=True) - xhat * jnp.mean(s * xhat, axis=1, keepdims=True)
            ) * inv
            acc[at, :] = grad
            hlow[at, :] = grad.astype(BF)
            small[0, 4:5, :] += col_sum(g * xhat)
            small[0, 5:6, :] += col_sum(g)
            small[0, 3:4, :] += col_sum(grad)
            return carry

        lax.fori_loop(0, rows // RB, norm_back, 0)
        for j in range(width // TILE):
            at = pl.ds(j * TILE, TILE)
            cg[:, at] = mm_nt(hlow[...], wo[at, :]).astype(BF)

        def back_state(p, carry):
            at = lanes(p)
            total = den[:, at]
            inv = 1.0 / jnp.maximum(total, 1.0)
            g = cg[:, at].astype(F32)
            numer = (g * inv).astype(BF)
            sums = mm(two_parts(g * num[:, at]), bb[...])
            den_grad = jnp.where(total > 1.0, -sums * inv, 0.0)
            ngr[:, at] = numer
            dgr[:, at] = den_grad
            qc, qs = feats(rq, p, 0)
            full = mm_tn(numer, jnp.concatenate([qc, qs], axis=1))
            state[p] = compact_of(full)
            ssum[0:1, at] = col_sum(qc.astype(F32) * den_grad)
            ssum[1:2, at] = col_sum(qs.astype(F32) * den_grad)
            return carry

        lax.fori_loop(0, PAIRS, back_state, 0)
        finish_forward()

        def back_local(p, carry):
            at = lanes(p)
            qp = rq[:, at]
            kp = rk[:, at]
            vp = vv[:, at]
            numer = ngr[:, at]
            den_grad = dgr[:, at]
            k2 = halves(kp)
            q2 = halves(qp)
            n2 = halves(numer)
            dh = den_grad.astype(BF)
            dl = (den_grad - dh.astype(F32)).astype(BF)
            x = dh * masks[2, :1] + dl * masks[3, :1]
            ds = (
                mm_nt(
                    jnp.concatenate([numer, x], axis=1),
                    jnp.concatenate([halves(vp), c1[...]], axis=1),
                )
                * m2[...]
            ).astype(BF)
            grad_q = mm(ds, k2)
            at_scores = (mm_nt(kp, q2) * mt2[...]).astype(BF)
            gv_part = mm(at_scores, n2)
            dst = (
                mm_nt(
                    jnp.concatenate([vp, ec[...]], axis=1),
                    jnp.concatenate([n2, halves(x)], axis=1),
                )
                * mt2[...]
            ).astype(BF)
            gk_part = mm(dst, q2)
            t = mm(numer, expand(state_in[p]))
            cq = cols[0]
            sq = cols[1]
            grad_q = grad_q + cq * t[:, :PAIR] + sq * t[:, PAIR:]
            grad_q = grad_q + den_grad * (cq * ssum_in[0:1, at] + sq * ssum_in[1:2, at])
            grad_q = jnp.where(qp.astype(F32) > 0.0, grad_q, 0.0)
            small[0, 0:1, at] = col_sum(grad_q)
            gq[:, at] = grad_q.astype(BF)
            normed[:, at] = gk_part
            hid[:, at] = gv_part
            return carry

        lax.fori_loop(0, PAIRS, back_local, 0)
        finish_backward = chain(grad_out, gsum_out, grad_in, gsum_in, state, ssum, False)

        tokt[...] = tok[...].T

        def weight_grad(index, left_t, right):
            def body(i, carry):
                at = rds(i * TILE, TILE, TILE)
                for j in range(width // TILE):
                    to = pl.ds(j * TILE, TILE)
                    part[rds(index * width + i * TILE, TILE, TILE), to] = mm(
                        left_t[at, :], right[:, to]
                    ).astype(BF)
                return carry

            lax.fori_loop(0, width // TILE, body, 0)

        weight_grad(0, tokt, gq)

        def back_remote(p, carry):
            at = lanes(p)
            full = expand(grad_in[p])
            t = mm(vv[:, at], full)
            kc, ks = feats(rk, p, 2)
            ck = cols[2]
            sk = cols[3]
            grad_k = normed[:, at] + ck * (t[:, :PAIR] + gsum_in[0:1, at]) + sk * (
                t[:, PAIR:] + gsum_in[1:2, at]
            )
            grad_k = jnp.where(rk[:, at].astype(F32) > 0.0, grad_k, 0.0)
            small[0, 1:2, at] = col_sum(grad_k)
            gk[:, at] = grad_k.astype(BF)
            grad_v = hid[:, at] + mm_nt(jnp.concatenate([kc, ks], axis=1), full)
            small[0, 2:3, at] = col_sum(grad_v)
            gv[:, at] = grad_v.astype(BF)
            return carry

        lax.fori_loop(0, PAIRS, back_remote, 0)
        weight_grad(1, tokt, gk)
        weight_grad(2, tokt, gv)
        tokt[...] = ctx[...].T
        weight_grad(3, tokt, hlow)

        def j_base(job, upto):
            base = 0
            for s in range(upto):
                base = base + bit(jobs[job][s]) * (width >> (s + 1))
            return base

        reds = [red0, red1, red2]
        rs_copies = {}

        def rs_start(job, s):
            half = width >> (s + 1)
            b = jobs[job][s]
            away = job * width + j_base(job, s) + (1 - bit(b)) * half
            copy = remote(part.at[rds(away, half)], reds[s].at[job], flip(b))
            copy.start()
            rs_copies[job, s] = copy

        def rs_finish(job, s):
            half = width >> (s + 1)
            rs_copies[job, s].wait()
            keep = job * width + j_base(job, s + 1)
            step = min(half, 96)

            def body(i, carry):
                at = rds(keep + i * step, step)
                part[at, :] = (
                    part[at, :].astype(F32) + reds[s][job, rds(i * step, step), :].astype(F32)
                ).astype(BF)
                return carry

            lax.fori_loop(0, half // step, body, 0)

        def extra(job):
            for e, b in enumerate(range(nhalf, nbits)):
                at = rds(job * width + j_base(job, nhalf), piece)
                copy = remote(part.at[at], redx.at[job, e], flip(b))
                copy.start()
                copy.wait()
                part[at, :] = (part[at, :].astype(F32) + redx[job, e].astype(F32)).astype(BF)

        def ag_copy(job, s):
            size = width >> (s + 1)
            at = rds(job * width + j_base(job, s + 1), size)
            return remote(gsum.at[at], gsum.at[at], flip(jobs[job][s]))

        def run_small():
            for b in range(nbits):
                copy = remote(small.at[b], smallr.at[b], flip(b))
                copy.start()
                copy.wait()
                small[b + 1] = small[b] + smallr[b]
            smallz[mp] = small[nbits]
            copies = [remote(smallz.at[mp], smallz.at[mp], peer(r)) for r in range(1, mp_size)]
            for copy in copies:
                copy.start()
            for copy in copies:
                copy.wait()
            total = smallz[0]
            for z in range(1, mp_size):
                total = total + smallz[z]
            smallr[0, 0:8] = total[0:8]
            keep_row = lax.broadcasted_iota(jnp.int32, (8, width), 0) == 7
            smallr[0, 8:16] = jnp.where(keep_row, small[nbits, 8:16], total[8:16])

        attn_jobs = list(range(4))
        for job in attn_jobs:
            rs_start(job, 0)

        for j in range(width // TILE):
            at = pl.ds(j * TILE, TILE)
            total = acc[:, at] + mm_nt(gq[...], wq[at, :]) + mm_nt(gk[...], wk[at, :])
            in_out[1, :, at] = (total + mm_nt(gv[...], wv[at, :])).astype(BF)
        input_copy = local(in_out.at[1], out_input)
        input_copy.start()

        for job in attn_jobs:
            rs_finish(job, 0)
            rs_start(job, 1)

        for copy in norm_copies:
            copy.wait()
        for copy in merged_copies:
            copy.wait()
        tiles = width // TILE
        gps[...] = jnp.zeros_like(gps)

        def shard_grads(c, carry):
            for j in range(shard // TILE):
                at = pl.ds(j * TILE, TILE)
                u = mm(nf[c], wu[mp, :, at]) + ub[mp, 0:1, at]
                value, slope = gelu_both(u)
                up_grad = mm_nt(mf[c], wd[mp, at, :]) * slope
                small[0, 15:16, at] += col_sum(up_grad)
                gq[:, at] = value.astype(BF)
                ulow[:, at] = up_grad.astype(BF)
            for j in range(tiles):
                at = pl.ds(j * TILE, TILE)
                gps[j] += mm_tn(nf[c, :, at], ulow[...])
                gps[tiles + j] += mm_tn(gq[:, at], mf[c])
            return carry

        lax.fori_loop(0, mp_size, shard_grads, 0)
        for index in range(2):
            for j in range(width // TILE):
                part[pl.ds((4 + index) * width + j * TILE, TILE), :] = gps[index * tiles + j].astype(BF)
        for job in (4, 5):
            rs_start(job, 0)
        for s in range(1, nhalf):
            for job in attn_jobs:
                rs_finish(job, s)
                if s + 1 < nhalf:
                    rs_start(job, s + 1)
            for job in (4, 5):
                rs_finish(job, s - 1)
                rs_start(job, s)
        for job in attn_jobs:
            extra(job)

        quarter = piece // 2

        def quarter_row(first, t):
            which = lax.div(t, 2)
            base = (1 - which) * j_base(first, nhalf) + which * j_base(first + 1, nhalf)
            return (first + which) * width + base + lax.rem(t, 2) * quarter

        z_copies = {}
        for first in (0, 2):
            z_copies[first] = []
            for r in range(1, mp_size):
                t = lax.rem(mp + r, mp_size)
                z_copies[first].append(
                    remote(part.at[rds(quarter_row(first, t), quarter)], zr.at[first // 2, r - 1], peer(r))
                )
            for copy in z_copies[first]:
                copy.start()
        for job in (4, 5):
            rs_finish(job, nhalf - 1)
            extra(job)
            at = rds(job * width + j_base(job, nhalf), piece)
            gsum[at, :] = part[at, :]
        ff_ag = [ag_copy(job, nhalf - 1) for job in (4, 5)]
        for copy in ff_ag:
            copy.start()
        z_back = {}
        for first in (0, 2):
            for copy in z_copies[first]:
                copy.wait()
            at = rds(quarter_row(first, mp), quarter)
            total = part[at, :].astype(F32)
            for r in range(mp_size - 1):
                total = total + zr[first // 2, r].astype(F32)
            gsum[at, :] = total.astype(BF)
            z_back[first] = [remote(gsum.at[at], gsum.at[at], peer(r)) for r in range(1, mp_size)]
            for copy in z_back[first]:
                copy.start()
        run_small()
        for first in (0, 2):
            for copy in z_back[first]:
                copy.wait()
        pending = {job: ff_ag[job - 4] for job in (4, 5)}
        for job in attn_jobs:
            pending[job] = ag_copy(job, nhalf - 1)
            pending[job].start()
        for s in range(nhalf - 2, -1, -1):
            for job in (4, 5, 0, 1, 2, 3):
                pending[job].wait()
                pending[job] = ag_copy(job, s)
                pending[job].start()
        for job in (4, 5, 0, 1, 2, 3):
            pending[job].wait()
        outs = [
            local(gsum.at[pl.ds(0, 4 * width)], out_attn),
            local(gsum.at[pl.ds(4 * width, 2 * width)], out_ff),
            local(smallr.at[0], out_small),
        ]
        for copy in outs:
            copy.start()
        finish_backward()
        layer_copy.wait()
        input_copy.wait()
        for copy in outs:
            copy.wait()

    def call(*operands):
        vm = pltpu.VMEM
        big = lambda *s: vm(s, BF)
        flt = lambda *s: vm(s, F32)
        nsem = 160
        scratch = [
            big(mp_size, width, shard), big(mp_size, shard, width), flt(mp_size, 8, shard),
            big(rows, width), big(rows, width), big(rows, width),
            flt(rows, 2 * rows), flt(rows, 2 * rows), flt(4, rows, 128),
            big(2 * rows, PAIR), big(2 * PAIR, PAIR), big(2 * rows, PAIR), big(rows, PAIR), big(4, 16, PAIR),
            flt(PAIRS, HD, 2 * PAIR), big(PAIRS, HD, 2 * PAIR), flt(8, width), flt(8, width),
            big(PAIRS, HD, 2 * PAIR), flt(8, width), big(PAIRS, HD, 2 * PAIR), flt(8, width),
            big(PAIRS, HD, 2 * PAIR), flt(8, width),
            flt(rows, width), flt(rows, width), big(rows, width), flt(rows, width), flt(rows, 128),
            flt(rows, width), big(mp_size, rows, width), big(mp_size, rows, width),
            big(mp_size, rows, shard), flt(2 * (width // TILE), rows, shard), flt(rows, width), flt(rows, width),
            big(rows, shard), big(rows, width), big(rows, width), big(rows, width), flt(rows, width),
            big(rows, width), big(rows, width), big(rows, width),
            big(6 * width, width), big(6 * width, width),
            big(6, width // 2, width), big(6, width // 4, width), big(6, width // 8, width),
            big(6, max(1, nbits - nhalf), piece, width), big(2, mp_size - 1, piece // 2, width),
            flt(nbits + 1, 16, width), flt(nbits, 16, width), flt(mp_size, 16, width),
            big(width, rows), big(2, rows, width),
            pltpu.SemaphoreType.DMA((16,)), pltpu.SemaphoreType.DMA((nsem,)), pltpu.SemaphoreType.DMA((nsem,)),
        ]
        spec = pl.BlockSpec(memory_space=pltpu.VMEM)
        anywhere = pl.BlockSpec(memory_space=pl.ANY)
        return pl.pallas_call(
            kernel,
            out_shape=(
                jax.ShapeDtypeStruct((rows, width), BF),
                jax.ShapeDtypeStruct((rows, width), BF),
                jax.ShapeDtypeStruct((4 * width, width), BF),
                jax.ShapeDtypeStruct((2 * width, width), BF),
                jax.ShapeDtypeStruct((16, width), F32),
            ),
            in_specs=[pl.BlockSpec(memory_space=pltpu.SMEM)] + [spec] * 7 + [anywhere] * 2,
            out_specs=(anywhere,) * 5,
            scratch_shapes=scratch,
            compiler_params=pltpu.CompilerParams(
                collective_id=0, has_side_effects=True, vmem_limit_bytes=62 * 1024 * 1024
            ),
        )(*operands)

    return call


def solution(mesh):
    dp_size, mp_size = mesh.shape["dp"], mesh.shape["mp"]

    def on_device(
        tokens, doc_starts, query_proj, key_proj, value_proj, query_bias, key_bias, value_bias,
        output_proj, output_bias, attn_gain, attn_shift, up_proj, up_bias, down_proj, down_bias,
        ffn_gain, ffn_shift, cotangent,
    ):
        _, rows, width = tokens.shape
        shard = up_proj.shape[1]
        blank = jnp.zeros((width,), F32)
        vec = jnp.stack(
            [query_bias, key_bias, value_bias, output_bias, attn_gain, attn_shift, down_bias,
             ffn_gain, ffn_shift] + [blank] * 6 + [up_bias]
        )
        call = build(dp_size, mp_size, rows, width, shard)
        layer_out, input_grad, attn, ff, small = call(
            doc_starts, tokens[0], cotangent[0], query_proj, key_proj, value_proj, output_proj,
            vec, up_proj, down_proj,
        )
        attn = attn.astype(F32).reshape(4, width, width)
        ff = ff.astype(F32).reshape(2, width, width)
        return (
            layer_out[None], input_grad[None], attn[0], attn[1], attn[2],
            small[0], small[1], small[2], attn[3], small[3], small[4], small[5],
            ff[0], small[15], ff[1], small[6], small[7], small[8],
        )

    rows_spec = P("dp", "mp", None)
    placed = (
        rows_spec, P("dp", None), P(), P(), P(), P(), P(), P(), P(), P(), P(), P(),
        P(None, "mp"), P("mp"), P("mp", None), P(), P(), P(), rows_spec,
    )
    results = (
        rows_spec, rows_spec, P(), P(), P(), P(), P(), P(), P(), P(), P(), P(),
        P(None, "mp"), P("mp"), P("mp", None), P(), P(), P(),
    )
    return jax.shard_map(
        on_device, mesh=mesh, in_specs=placed, out_specs=results, check_vma=False
    )
```

time: 809 us -> 249 us (0.31)
  waiting for transfers between devices: 400 us -> 0 us
  Pallas kernels: 0 us -> 226 us
  local copies, waits for them, and re-layouts: 144 us -> 19.8 us
  matrix products: 115 us -> 0 us
  other arithmetic: 71.9 us -> 0 us
  blocking collectives: 54.7 us -> 0 us
  between operations: 15.3 us -> 0.68 us
    pallas_call x0 -> x1, Pallas kernels: none -> 226 us  [call(): pl.pallas_call(kernel, out_shape=(jax.ShapeDtypeStruct((rows, width), BF)...]
    psum x2 -> x0, waiting for transfers between devices: 198 us -> none  [the longest x1 121 us: on_device(): lax.psum((proj_grads, proj_bias, output_proj_grad, output_bias_grad, attn...]
    all_gather x4 -> x0, waiting for transfers between devices: 133 us -> none  [the longest x1 36.2 us: on_device(): lax.all_gather(merged_grad.astype(jnp.bfloat16), 'mp', axis=1, tiled=True)]
    dot_general x30 -> x0, matrix products: 115 us -> none  [the longest x3 12.5 us: rowwise(): jnp.einsum('rlk,kn->rln', left, right, preferred_element_type=jnp.float32)]
    reduce_scatter x2 -> x0, waiting for transfers between devices: 68.5 us -> none  [the longest x1 34.3 us: on_device(): lax.psum_scatter(jnp.einsum('rlf,df->lrd', piece, up_proj, preferred_elem...]
    psum x2 -> x0, blocking collectives: 54.7 us -> none  [the longest x1 40.4 us: on_device(): lax.psum((proj_grads, proj_bias, output_proj_grad, output_bias_grad, attn...]
    reshape x5 -> x0, local copies, waits for them, and re-layouts: 30.6 us -> none  [the longest x4 24.7 us: features(): head_vals = jax.nn.relu(pre_act).reshape(batch_rows, length, HEADS, HD)]
    convert_element_type x6 -> x0, local copies, waits for them, and re-layouts: 28 us -> none  [the longest x4 22.1 us: attend_back(): grad_vals = context_grad.astype(jnp.float32)]
  transfers between devices with their start and end apart: 8 -> 0, of which waited for: 8 -> 0; matrix products, arithmetic and copies ran while one was open for 6% -> 0% of each run, Pallas kernels for 0% -> 0%
where the time goes in v1:
time: 249 us; the launch traced here: 247 us
  Pallas kernels  226 us (91%)
  local copies, waits for them, and re-layouts  19.8 us (8%)
    pallas_call x1, Pallas kernels, call(): pl.pallas_call(kernel, out_shape=(jax.ShapeDtypeStruct((rows, width), BF)...  226 us
    slice x1, local copies, waits for them, and re-layouts, on_device(): attn[3]  8.37 us
    another operation x13, local copies, waits for them, and re-layouts, on_device(): jnp.stack([query_bias, key_bias, value_bias, output_bias, attn_gain, attn...  8.18 us

profile of v1, /device:TPU:0, one launch (start us, length us, event | category | flops | bytes accessed | tf_op | source)
XLA Modules:
  0.0 246.6 jit_solution(11372039473546098490)
XLA Ops:
  0.7 0.7 stack.39
  1.3 0.7 stack.40
  2.0 0.7 stack.41
  2.7 0.7 stack.42
  3.4 0.7 stack.43
  4.1 0.7 stack.44
  4.8 0.7 stack.50
  5.5 0.7 stack.45
  6.2 0.7 stack.46
  6.9 0.7 stack.47
  7.6 1.3 stack.51.vec
  8.8 226.1 %shard_map.322 = (bf16[256,768]{1,0:T(8,128)(2,1)}, bf16[256,768]{1,0:T(8,128)(2,1)}, bf16[3072,768]{1,0:T(8,128)(2,1)}, bf16[1536,768]{1,0:T(8,128)(2,1)}, f32[16,768]{1,0:T(8,128)}) custom-call(s32[1,2]{1,0:T(1,128)} %starts.1, bf16[256,768]{1,0:T(8,128)(2,1)} %bitcast.4, bf16[256,768]{1,0:T(8,128)(2,1)} %bitcast.5, bf16[768,768]{1,0:T(8,128)(2,1)} %wq.1, ...), custom_call_target="tpu_custom_call" | custom-call | tf_op jit(solution)/shard_map/pallas_call | solution.py:761
  235.0 1.7 slice_reduce_fusion
  236.7 0.0 copy-start.1
  236.7 0.0 copy-start
  236.7 8.4 %fusion = (f32[768,768]{1,0:T(8,128)}, f32[768,768]{1,0:T(8,128)}, f32[768,768]{1,0:T(8,128)}, f32[768,768]{1,0:T(8,128)}, f32[768,768]{1,0:T(8,128)}, /*index=5*/f32[768,768]{1,0:T(8,128)}) fusion(bf16[3072,768]{1,0:T(8,128)(2,1)} %get-tuple-element.25, bf16[1536,768]{1,0:T(8,128)(2,1)} %get-tuple-element.27), kind=kLoop, calls=%fused_computation.10 | loop fusion | bytes 28311552 | tf_op jit(solution)/shard_map/slice | solution.py:805
  245.1 0.0 copy-done.1
  245.1 0.7 copy.39
  245.9 0.0 copy-done
  245.9 0.7 copy.40
  (2 shorter events, 0.0 us)
Async XLA Ops:
  236.7 8.4 %copy-start.1 = (bf16[256,768]{1,0:T(8,128)(2,1)S(1)}, bf16[256,768]{1,0:T(8,128)(2,1)}, u32[]{:S(2)}) copy-start(bf16[256,768]{1,0:T(8,128)(2,1)} %get-tuple-element.23) | copy-start | bytes 1179652
  236.7 9.1 %copy-start = (bf16[256,768]{1,0:T(8,128)(2,1)S(1)}, bf16[256,768]{1,0:T(8,128)(2,1)}, u32[]{:S(2)}) copy-start(bf16[256,768]{1,0:T(8,128)(2,1)} %get-tuple-element.24) | copy-start | bytes 1179652

commit v2 on v1

v2 whole, which is shorter than its diff:
```python
import math

import jax
import jax.numpy as jnp
from jax import lax
from jax.experimental import pallas as pl
from jax.experimental.pallas import tpu as pltpu
from jax.sharding import PartitionSpec as P

HEADS = 12
HD = 64
SEQ = 1024
DOCS = 2
PAIR = 2 * HD
PAIRS = HEADS // 2
TILE = 256
MESH = pl.DeviceIdType.MESH
BF = jnp.bfloat16
F32 = jnp.float32
C0 = math.sqrt(2.0 / math.pi)
C1 = 0.044715


def mm(a, b):
    return lax.dot_general(a, b, (((1,), (0,)), ((), ())), preferred_element_type=F32)


def mm_nt(a, b):
    return lax.dot_general(a, b, (((1,), (1,)), ((), ())), preferred_element_type=F32)


def mm_tn(a, b):
    return lax.dot_general(a, b, (((0,), (0,)), ((), ())), preferred_element_type=F32)


def gelu_both(u):
    square = u * u
    t = jnp.tanh(C0 * u * (1.0 + C1 * square))
    half = 0.5 * (1.0 + t)
    slope = half + (0.5 * C0) * u * (1.0 - t * t) * (1.0 + (3.0 * C1) * square)
    return u * half, slope


def two_parts(x):
    high = x.astype(BF)
    return jnp.concatenate([high, (x - high.astype(F32)).astype(BF)], axis=1)


def col_sum(x):
    return jnp.sum(x, axis=0, keepdims=True)


def build(dp_size, mp_size, rows, width, shard):
    nbits = dp_size.bit_length() - 1
    nhalf = min(3, nbits)
    piece = width >> nhalf

    def order(kind):
        first = list(range(nhalf))
        if kind == 1 and nhalf == 3:
            first = [0, 2, 1]
        return first

    def w_order(kind):
        plain = order(kind)
        return plain[1:] + plain[:1]

    jobs = [order(k % 2) for k in range(8)]

    def kernel(
        starts, b_q, b_k, b_v, b_o, g_a, s_a, b_d, g_f, s_f, b_u,
        tok_hbm, cot_hbm, wq_hbm, wk_hbm, wv_hbm, wo_hbm, up_hbm, down_hbm,
        out_layer, out_input, out_q, out_k, out_v, out_o, out_up, out_down, out_small,
        tok, cot, wq, wk, wv, wo, vec, wu, wd, ub, rq, rk, vv, m2, mt2, cols, o2, bb, c1, ec, masks,
        state, state_in, ssum, ssum_in, grad_in, gsum_in, state_out, ssum_out, gsum_out,
        num, den, ctx, hid, rstd, normed, nf, mf, acted, gps, act2, upl2, zf, acc, mg, hlow, ngr,
        gq, gk, gv, part, gsum, red0, red1, red2, redx, zr, small, smallr, smallz, tokt, in_out,
        local_sem, send_sem, recv_sem,
    ):
        dp = lax.axis_index("dp")
        mp = lax.axis_index("mp")
        counter = [0]
        locals_used = [0]

        def bit(b):
            return lax.rem(lax.div(dp, 1 << b), 2)

        def flip(b):
            return {"dp": dp + (1 - 2 * bit(b)) * (1 << b)}

        def peer(r):
            return {"mp": lax.rem(mp + r, mp_size)}

        def across(i):
            other, span = mp, 1
            while span < mp_size:
                if i & span:
                    other = other + span * (1 - 2 * lax.rem(lax.div(mp, span), 2))
                span *= 2
            return other

        def remote(src, dst, device):
            i = counter[0]
            counter[0] += 1
            return pltpu.make_async_remote_copy(
                src_ref=src, dst_ref=dst, send_sem=send_sem.at[i], recv_sem=recv_sem.at[i],
                device_id=device, device_id_type=MESH,
            )

        def local(src, dst):
            i = locals_used[0]
            locals_used[0] += 1
            return pltpu.make_async_copy(src, dst, local_sem.at[i])

        def rds(start, size, unit=16):
            return pl.ds(pl.multiple_of(start, unit), size)

        barrier = pltpu.get_barrier_semaphore()
        for b in range(nbits):
            pl.semaphore_signal(barrier, inc=1, device_id=flip(b), device_id_type=MESH)
        for r in range(1, mp_size):
            pl.semaphore_signal(barrier, inc=1, device_id=peer(r), device_id_type=MESH)
        loads = {}
        for name, src, dst in (
            ("tok", tok_hbm, tok), ("q", wq_hbm, wq), ("k", wk_hbm, wk), ("v", wv_hbm, wv),
            ("o", wo_hbm, wo), ("up", up_hbm, wu.at[mp]), ("down", down_hbm, wd.at[mp]), ("cot", cot_hbm, cot),
        ):
            loads[name] = local(src, dst)
            loads[name].start()
        for index, source in enumerate((b_q, b_k, b_v, b_o, g_a, s_a, b_d, g_f, s_f)):
            vec[index : index + 1, :] = source[...].reshape(1, width)
        vec[15:16, :] = b_u[...].reshape(1, shard)
        ub[mp] = jnp.broadcast_to(vec[15:16, :], (8, shard))
        def w_base(kind, upto):
            bits = w_order(kind)
            base = 0
            for s in range(nhalf - 1, upto - 1, -1):
                base = base + bit(bits[s]) * (piece << s)
            return base

        half_cols = shard // 2

        def weight_job(kind, i, side):
            source, buf = ((up_hbm, wu), (down_hbm, wd))[kind]
            cols_at = pl.ds(side * half_cols, half_cols)
            at = rds(w_base(side, 0), piece)
            copy = remote(source.at[at, cols_at], buf.at[mp, at, cols_at], {"mp": across(i)})
            copy.start()
            yield
            for s in range(nhalf):
                copy.wait()
                ref = buf.at[across(i), rds(w_base(side, s), piece << s), cols_at]
                copy = remote(ref, ref, flip(w_order(side)[s]))
                copy.start()
                yield
            copy.wait()
            yield

        weight_jobs = {
            (kind, i, side): weight_job(kind, i, side)
            for kind in (0, 1) for i in range(1, mp_size) for side in (0, 1)
        }

        def pump(kind, which=range(1, mp_size)):
            for i in which:
                for side in (0, 1):
                    next(weight_jobs[kind, i, side])

        own_start = mp * rows

        def layout(places):
            opened = jnp.full(places.shape, 0, jnp.int32) + starts[0, 0]
            closed = jnp.full(places.shape, SEQ, jnp.int32)
            if DOCS > 1:
                closed = jnp.full(places.shape, 0, jnp.int32) + starts[0, 1]
            number = jnp.zeros(places.shape, jnp.int32)
            for d in range(1, DOCS):
                ending = starts[0, d + 1] if d + 1 < DOCS else SEQ
                inside = places >= starts[0, d]
                opened = jnp.where(inside, starts[0, d], opened)
                closed = jnp.where(inside, ending, closed)
                number = number + inside.astype(jnp.int32)
            angles = (places - opened).astype(F32) * (0.5 * math.pi) / (closed - opened).astype(F32)
            return number, jnp.cos(angles), jnp.sin(angles)

        places = own_start + lax.broadcasted_iota(jnp.int32, (rows, 128), 0)
        number_c, cos_c, sin_c = layout(places)
        row_places = own_start + lax.broadcasted_iota(jnp.int32, (8, rows), 1)
        number_r, cos_r, sin_r = layout(row_places)
        edge = jnp.zeros((8, 128), jnp.int32)
        last, _, _ = layout(edge + own_start + (rows - 1))
        before, _, _ = layout(edge + own_start - 1)
        has_prev = jnp.where(edge + mp > 0, 1.0, 0.0)
        carried = jnp.where(number_c == before[:1], 1.0, 0.0) * has_prev[:1]
        in_last = jnp.where(number_c == last[:1], 1.0, 0.0)
        linked = (jnp.where(before == last, 1.0, 0.0) * has_prev)[:1]
        cols[0] = cos_c * carried
        cols[1] = sin_c * carried
        cols[2] = cos_c * in_last
        cols[3] = sin_c * in_last
        linked2 = jnp.concatenate([linked, linked], axis=1)
        linked6 = jnp.concatenate([linked] * (width // 128), axis=1)
        wide = jnp.concatenate([number_c, number_c], axis=1)
        wide_cos = jnp.concatenate([cos_c, cos_c], axis=1)
        wide_sin = jnp.concatenate([sin_c, sin_c], axis=1)
        row_id = lax.broadcasted_iota(jnp.int32, (rows, rows), 0)
        col_id = lax.broadcasted_iota(jnp.int32, (rows, rows), 1)
        angle_gap = wide_cos * cos_r[:1] + wide_sin * sin_r[:1]
        same = wide == number_r[:1]
        lower = jnp.where(same & (col_id <= row_id), angle_gap, 0.0)
        upper_part = jnp.where(same & (col_id >= row_id), angle_gap, 0.0)
        m2[:, :rows] = lower
        m2[:, rows:] = lower
        mt2[:, :rows] = upper_part
        mt2[:, rows:] = upper_part

        lane = lax.broadcasted_iota(jnp.int32, (rows, PAIR), 1)
        low_f = jnp.where(lane < HD, 1.0, 0.0)
        high_f = 1.0 - low_f
        first_two = jnp.where(lax.rem(lane, HD) < 2, 1.0, 0.0)
        o2[:rows, :] = low_f.astype(BF)
        o2[rows:, :] = high_f.astype(BF)
        c1[:rows, :] = (first_two * low_f).astype(BF)
        c1[rows:, :] = (first_two * high_f).astype(BF)
        ec[...] = first_two.astype(BF)
        block_row = lax.broadcasted_iota(jnp.int32, (2 * PAIR, PAIR), 0)
        block_col = lax.broadcasted_iota(jnp.int32, (2 * PAIR, PAIR), 1)
        bb[...] = jnp.where(
            lax.div(lax.rem(block_row, PAIR), HD) == lax.div(block_col, HD), 1.0, 0.0
        ).astype(BF)
        lo = low_f.astype(BF)[:16]
        hi = high_f.astype(BF)[:16]
        masks[0] = lo
        masks[1] = hi
        masks[2] = jnp.where(lax.rem(lane, HD) == 0, 1.0, 0.0).astype(BF)[:16]
        masks[3] = jnp.where(lax.rem(lane, HD) == 1, 1.0, 0.0).astype(BF)[:16]

        def halves(x):
            return jnp.concatenate([x * masks[0, :1], x * masks[1, :1]], axis=0)

        def expand(compact):
            low4 = jnp.concatenate([masks[0, :1]] * 2, axis=1)
            high4 = jnp.concatenate([masks[1, :1]] * 2, axis=1)
            return jnp.concatenate([compact * low4, compact * high4], axis=0)

        def compact_of(full):
            low4 = jnp.concatenate([masks[0, :1]] * 2, axis=1).astype(F32)
            high4 = jnp.concatenate([masks[1, :1]] * 2, axis=1).astype(F32)
            return full[:HD] * low4 + full[HD:] * high4

        def project(weight, out, name, row):
            loads[name].wait()
            for j in range(width // TILE):
                at = pl.ds(j * TILE, TILE)
                y = mm(tok[...], weight[:, at]) + vec[row : row + 1, at]
                if row < 2:
                    y = jnp.maximum(y, 0.0)
                out[:, at] = y.astype(BF)

        loads["tok"].wait()
        project(wk, rk, "k", 1)
        project(wv, vv, "v", 2)

        def lanes(p):
            return pl.ds(pl.multiple_of(p * PAIR, PAIR), PAIR)

        def feats(ref, p, which):
            x = ref[:, lanes(p)].astype(F32)
            return (x * cols[which]).astype(BF), (x * cols[which + 1]).astype(BF)

        def contribs(p, carry):
            kc, ks = feats(rk, p, 2)
            full = mm_tn(vv[:, lanes(p)], jnp.concatenate([kc, ks], axis=1))
            state[p] = compact_of(full)
            ssum[0:1, lanes(p)] = col_sum(kc.astype(F32))
            ssum[1:2, lanes(p)] = col_sum(ks.astype(F32))
            return carry

        ssum[...] = jnp.zeros_like(ssum)
        lax.fori_loop(0, PAIRS, contribs, 0)

        CH = 3
        PC = PAIRS // CH

        class Chain:
            def __init__(self, out_state, out_sum, in_state, in_sum, forward):
                step = 1 if forward else mp_size - 1
                self.has_in = (mp > 0) if forward else (mp < mp_size - 1)
                self.has_out = (mp < mp_size - 1) if forward else (mp > 0)
                self.rank = mp if forward else mp_size - 1 - mp
                self.refs = out_state, out_sum, in_state, in_sum
                self.copies = [
                    remote(out_state.at[pl.ds(c * PC, PC)], in_state.at[pl.ds(c * PC, PC)], peer(step))
                    for c in range(CH)
                ]
                self.sum_copy = remote(out_sum, in_sum, peer(step))

            def early(self):
                out_state, out_sum, in_state, in_sum = self.refs

                @pl.when(jnp.logical_not(self.has_in))
                def _():
                    in_state[...] = jnp.zeros_like(in_state)
                    in_sum[...] = jnp.zeros_like(in_sum)
                    out_sum[...] = ssum[...]
                    self.sum_copy.start()
                    for c in range(CH):
                        at = pl.ds(c * PC, PC)
                        out_state[at] = state[at].astype(BF)
                        self.copies[c].start()

            def slot(self, k):
                for c in range(CH):
                    if 0 <= k - c <= mp_size - 2:
                        self.service(c, self.rank == k - c + 1)

            def service(self, c, here):
                out_state, out_sum, in_state, in_sum = self.refs

                @pl.when(here)
                def _():
                    if c == 0:
                        self.sum_copy.wait_recv()

                        @pl.when(self.has_out)
                        def _():
                            out_sum[...] = ssum[...] + in_sum[...] * linked6
                            self.sum_copy.start()

                    self.copies[c].wait_recv()

                    @pl.when(self.has_out)
                    def _():
                        for p in range(c * PC, (c + 1) * PC):
                            out_state[p] = (state[p] + in_state[p].astype(F32) * linked2).astype(BF)
                        self.copies[c].start()

            def finish(self):
                @pl.when(self.has_out)
                def _():
                    for copy in self.copies + [self.sum_copy]:
                        copy.wait_send()

        ahead = Chain(state_out, ssum_out, state_in, ssum_in, True)
        behind = Chain(state_out, gsum_out, grad_in, gsum_in, False)
        neighbour = {"mp": across(1)}
        norm_pair = remote(nf.at[pl.ds(0, rows)], nf.at[pl.ds(rows, rows)], neighbour)
        merged_pair = remote(mf.at[pl.ds(0, rows)], mf.at[pl.ds(rows, rows)], neighbour)
        pl.semaphore_wait(barrier, nbits + mp_size - 1)
        pump(0)
        ahead.early()
        bias_copies = [remote(ub.at[mp], ub.at[mp], {"mp": across(i)}) for i in range(1, mp_size)]
        for copy in bias_copies:
            copy.start()
        project(wq, rq, "q", 0)
        flow = [(k, i) for k in (0, 1) for i in range(1, mp_size)]

        def wave(d):
            for stage in range(nhalf + 1):
                if 0 <= d - stage < len(flow):
                    kind, i = flow[d - stage]
                    pump(kind, [i])

        def local_attention(p, carry):
            k2 = halves(rk[:, lanes(p)])
            a = (mm_nt(rq[:, lanes(p)], k2) * m2[...]).astype(BF)
            both = mm(a, jnp.concatenate([halves(vv[:, lanes(p)]), o2[...]], axis=1))
            num[:, lanes(p)] = both[:, :PAIR]
            den[:, lanes(p)] = both[:, PAIR:]
            return carry

        for c in range(CH):
            lax.fori_loop(c * PC, (c + 1) * PC, local_attention, 0)
            wave(c)
            pump(1, [c + 1])
            ahead.slot(c)
        wave(3)
        ahead.slot(3)
        wave(4)
        ahead.slot(4)

        def remote_attention(p, carry):
            at = lanes(p)
            qc, qs = feats(rq, p, 0)
            carry_num = mm_nt(jnp.concatenate([qc, qs], axis=1), expand(state_in[p]))
            weighted = qc.astype(F32) * ssum_in[0:1, at] + qs.astype(F32) * ssum_in[1:2, at]
            total = den[:, at] + mm(two_parts(weighted), bb[...])
            value = (num[:, at] + carry_num) / jnp.maximum(total, 1.0)
            den[:, at] = total
            num[:, at] = value
            ctx[:, at] = value.astype(BF)
            return carry

        lax.fori_loop(0, PAIRS, remote_attention, 0)

        loads["o"].wait()
        for j in range(width // TILE):
            at = pl.ds(j * TILE, TILE)
            hid[:, at] = tok[:, at].astype(F32) + mm(ctx[...], wo[:, at]) + vec[3:4, at]
        RB = 64

        def first_norm(i, carry):
            at = pl.ds(pl.multiple_of(i * RB, RB), RB)
            x = hid[at, :]
            center = x - jnp.mean(x, axis=1, keepdims=True)
            inv = lax.rsqrt(jnp.mean(center * center, axis=1, keepdims=True) + 1e-05)
            xhat = center * inv
            y = xhat * vec[4:5, :] + vec[5:6, :]
            hid[at, :] = xhat
            rstd[at, :] = jnp.broadcast_to(inv, (RB, 128))
            normed[at, :] = y
            nf[at, :] = y.astype(BF)
            return carry

        lax.fori_loop(0, rows // RB, first_norm, 0)
        norm_pair.start()

        def ffn_up(t):
            for j in range(shard // TILE):
                at = pl.ds(j * TILE, TILE)
                u = mm(nf[:rows, :], wu[t, :, at]) + ub[t, 0:1, at]
                value, slope = gelu_both(u)
                acted[t, :, at] = value.astype(BF)
                gps[t, :, at] = slope

        def ffn_down(t, first):
            for j in range(width // TILE):
                at = pl.ds(j * TILE, TILE)
                y = mm(acted[t], wd[t, :, at])
                if first:
                    acc[:, at] = y
                else:
                    acc[:, at] += y

        loads["up"].wait()
        loads["down"].wait()
        for copy in bias_copies:
            copy.wait()
        ffn_up(mp)
        wave(5)
        ffn_up(across(1))
        ffn_up(across(2))
        ffn_up(across(3))
        ffn_down(mp, True)
        wave(6)
        ffn_down(across(1), False)
        wave(7)
        ffn_down(across(2), False)
        wave(8)
        ffn_down(across(3), False)
        small[0] = jnp.zeros_like(small[0])
        loads["cot"].wait()

        def second_norm(i, carry):
            at = pl.ds(pl.multiple_of(i * RB, RB), RB)
            x = normed[at, :] + acc[at, :] + vec[6:7, :]
            center = x - jnp.mean(x, axis=1, keepdims=True)
            inv = lax.rsqrt(jnp.mean(center * center, axis=1, keepdims=True) + 1e-05)
            xhat = center * inv
            in_out[0, at, :] = (xhat * vec[7:8, :] + vec[8:9, :]).astype(BF)
            g = cot[at, :].astype(F32)
            s = g * vec[7:8, :]
            grad = (
                s - jnp.mean(s, axis=1, keepdims=True) - xhat * jnp.mean(s * xhat, axis=1, keepdims=True)
            ) * inv
            mg[at, :] = grad
            mf[at, :] = grad.astype(BF)
            small[0, 7:8, :] += col_sum(g * xhat)
            small[0, 8:9, :] += col_sum(g)
            small[0, 6:7, :] += col_sum(grad)
            return carry

        lax.fori_loop(0, rows // RB, second_norm, 0)
        layer_copy = local(in_out.at[0], out_layer)
        layer_copy.start()
        merged_pair.start()

        def ffn_back(r, carry):
            t = lax.rem(mp + r, mp_size)
            for j in range(shard // TILE):
                at = pl.ds(j * TILE, TILE)
                up_grad = mm_nt(mf[:rows, :], wd[t, at, :]) * gps[t, :, at]
                upl2[:rows, at] = up_grad.astype(BF)
            for j in range(width // TILE):
                at = pl.ds(j * TILE, TILE)
                mg[:, at] += mm_nt(upl2[:rows, :], wu[t, at, :])
            return carry

        lax.fori_loop(0, mp_size, ffn_back, 0)

        def norm_back(i, carry):
            at = pl.ds(pl.multiple_of(i * RB, RB), RB)
            g = mg[at, :]
            xhat = hid[at, :]
            s = g * vec[4:5, :]
            inv = rstd[at, 0:1]
            grad = (
                s - jnp.mean(s, axis=1, keepdims=True) - xhat * jnp.mean(s * xhat, axis=1, keepdims=True)
            ) * inv
            acc[at, :] = grad
            hlow[at, :] = grad.astype(BF)
            small[0, 4:5, :] += col_sum(g * xhat)
            small[0, 5:6, :] += col_sum(g)
            small[0, 3:4, :] += col_sum(grad)
            return carry

        lax.fori_loop(0, rows // RB, norm_back, 0)
        for j in range(width // TILE):
            at = pl.ds(j * TILE, TILE)
            gv[:, at] = mm_nt(hlow[...], wo[at, :]).astype(BF)

        def back_state(p, carry):
            at = lanes(p)
            total = den[:, at]
            inv = 1.0 / jnp.maximum(total, 1.0)
            g = gv[:, at].astype(F32)
            numer = (g * inv).astype(BF)
            sums = mm(two_parts(g * num[:, at]), bb[...])
            den_grad = jnp.where(total > 1.0, -sums * inv, 0.0)
            ngr[:, at] = numer
            mg[:, at] = den_grad
            qc, qs = feats(rq, p, 0)
            full = mm_tn(numer, jnp.concatenate([qc, qs], axis=1))
            state[p] = compact_of(full)
            ssum[0:1, at] = col_sum(qc.astype(F32) * den_grad)
            ssum[1:2, at] = col_sum(qs.astype(F32) * den_grad)
            return carry

        ssum[...] = jnp.zeros_like(ssum)
        ahead.finish()
        lax.fori_loop(0, PAIRS, back_state, 0)
        behind.early()

        def weight_grad(index, left_t, right):
            def body(i, carry):
                at = rds(i * TILE, TILE, TILE)
                for j in range(width // TILE):
                    to = pl.ds(j * TILE, TILE)
                    part[rds(index * width + i * TILE, TILE, TILE), to] = mm(
                        left_t[at, :], right[:, to]
                    ).astype(BF)
                return carry

            lax.fori_loop(0, width // TILE, body, 0)


        def j_base(job, upto):
            base = 0
            for s in range(upto):
                base = base + bit(jobs[job][s]) * (width >> (s + 1))
            return base

        reds = [red0, red1, red2]

        def part_of(job):
            if job < 4:
                return part.at[pl.ds(job * width, width)]
            return (wu, wd)[job % 2].at[across((1, 3)[(job - 4) // 2])]

        def add_rows(ref, start, count, received):
            step = min(count, 96)

            def body(i, carry):
                at = rds(start + i * step, step)
                ref[at, :] = (
                    ref[at, :].astype(F32) + received[rds(i * step, step), :].astype(F32)
                ).astype(BF)
                return carry

            lax.fori_loop(0, count // step, body, 0)

        def scatter_job(job):
            ref = part_of(job)
            for s in range(nhalf):
                half = width >> (s + 1)
                b = jobs[job][s]
                away = j_base(job, s) + (1 - bit(b)) * half
                copy = remote(ref.at[rds(away, half)], reds[s].at[job], flip(b))
                copy.start()
                yield
                copy.wait()
                add_rows(ref, j_base(job, s + 1), half, reds[s].at[job])
            for e, b in enumerate(range(nhalf, nbits)):
                at = rds(j_base(job, nhalf), piece)
                copy = remote(ref.at[at], redx.at[job, e], flip(b))
                copy.start()
                copy.wait()
                add_rows(ref, j_base(job, nhalf), piece, redx.at[job, e])
            yield

        outs = [out_q, out_o, out_v, out_k, out_up, out_down]
        final_copies = []

        def gather_job(job):
            for s in range(nhalf - 1, -1, -1):
                at = rds(job * width + j_base(job, s + 1), width >> (s + 1))
                copy = remote(gsum.at[at], gsum.at[at], flip(jobs[job][s]))
                copy.start()
                yield
                copy.wait()
            out = local(gsum.at[pl.ds(job * width, width)], outs[job])
            out.start()
            final_copies.append(out)
            yield

        quarter = piece // 2

        def quarter_row(first, t):
            which = lax.div(t, 2)
            base = (1 - which) * j_base(first, nhalf) + which * j_base(first + 1, nhalf)
            return (first + which) * width + base + lax.rem(t, 2) * quarter

        def z_job(first, slot):
            copies = []
            for i in range(1, mp_size):
                copies.append(
                    remote(
                        part.at[rds(quarter_row(first, across(i)), quarter)],
                        zr.at[slot, i - 1], {"mp": across(i)},
                    )
                )
                copies[-1].start()
            yield
            for copy in copies:
                copy.wait()
            at = rds(quarter_row(first, mp), quarter)
            total = part[at, :].astype(F32)
            for i in range(mp_size - 1):
                total = total + zr[slot, i].astype(F32)
            gsum[at, :] = total.astype(BF)
            copies = [remote(gsum.at[at], gsum.at[at], {"mp": across(i)}) for i in range(1, mp_size)]
            for copy in copies:
                copy.start()
            yield
            for copy in copies:
                copy.wait()
            yield

        def small_job():
            for b in range(nbits):
                copy = remote(small.at[b], smallr.at[b], flip(b))
                copy.start()
                yield
                copy.wait()
                small[b + 1] = small[b] + smallr[b]
            smallz[mp] = small[nbits]
            copies = [remote(smallz.at[mp], smallz.at[mp], {"mp": across(i)}) for i in range(1, mp_size)]
            for copy in copies:
                copy.start()
            yield
            for copy in copies:
                copy.wait()
            total = smallz[0]
            for z in range(1, mp_size):
                total = total + smallz[z]
            smallr[0, 0:8] = total[0:8]
            smallr[0, 8:16] = total[8:16]
            smallr[0, 15:16] = smallz[mp, 15:16] + smallz[across(2), 14:15]
            out = local(smallr.at[0], out_small)
            out.start()
            final_copies.append(out)
            yield

        def ff_z_job():
            copies = []
            for slot, job in enumerate((UB, DB)):
                at = rds(j_base(job, nhalf), piece)
                copies.append(remote(part_of(job).at[at], zf.at[slot], {"mp": across(2)}))
                copies[-1].start()
            yield
            for copy in copies:
                copy.wait()
            for slot, job in enumerate((UA, DA)):
                total = part_of(job)[rds(j_base(job, nhalf), piece), :].astype(F32) + zf[slot].astype(F32)
                gsum[rds(job * width + j_base(job, nhalf), piece), :] = total.astype(BF)
            yield

        Q, O, V, K, UA, DA, UB, DB = range(8)
        ff_z = ff_z_job()
        scatter = [scatter_job(job) for job in range(8)]
        gather = [gather_job(job) for job in range(6)]
        z_first = z_job(Q, 0)
        z_second = z_job(V, 1)
        smalls = small_job()

        def step(*generators):
            for g in generators:
                assert next(g, 1) is None

        tokt[...] = ctx[...].T
        weight_grad(O, tokt, hlow)
        step(scatter[O])

        def back_local(p, carry):
            at = lanes(p)
            qp = rq[:, at]
            kp = rk[:, at]
            vp = vv[:, at]
            numer = ngr[:, at]
            den_grad = mg[:, at]
            k2 = halves(kp)
            q2 = halves(qp)
            n2 = halves(numer)
            dh = den_grad.astype(BF)
            dl = (den_grad - dh.astype(F32)).astype(BF)
            x = dh * masks[2, :1] + dl * masks[3, :1]
            ds = (
                mm_nt(
                    jnp.concatenate([numer, x], axis=1),
                    jnp.concatenate([halves(vp), c1[...]], axis=1),
                )
                * m2[...]
            ).astype(BF)
            grad_q = mm(ds, k2)
            at_scores = (mm_nt(kp, q2) * mt2[...]).astype(BF)
            gv_part = mm(at_scores, n2)
            dst = (
                mm_nt(
                    jnp.concatenate([vp, ec[...]], axis=1),
                    jnp.concatenate([n2, halves(x)], axis=1),
                )
                * mt2[...]
            ).astype(BF)
            gk_part = mm(dst, q2)
            t = mm(numer, expand(state_in[p]))
            cq = cols[0]
            sq = cols[1]
            grad_q = grad_q + cq * t[:, :PAIR] + sq * t[:, PAIR:]
            grad_q = grad_q + den_grad * (cq * ssum_in[0:1, at] + sq * ssum_in[1:2, at])
            grad_q = jnp.where(qp.astype(F32) > 0.0, grad_q, 0.0)
            small[0, 0:1, at] = col_sum(grad_q)
            gq[:, at] = grad_q.astype(BF)
            normed[:, at] = gk_part
            hid[:, at] = gv_part
            return carry

        for c in range(CH):
            lax.fori_loop(c * PC, (c + 1) * PC, back_local, 0)
            behind.service(c, behind.has_in)
        step(scatter[O])
        tokt[...] = tok[...].T
        weight_grad(Q, tokt, gq)
        step(scatter[Q])

        def back_remote(p, carry):
            at = lanes(p)
            full = expand(grad_in[p])
            t = mm(vv[:, at], full)
            kc, ks = feats(rk, p, 2)
            ck = cols[2]
            sk = cols[3]
            grad_k = normed[:, at] + ck * (t[:, :PAIR] + gsum_in[0:1, at]) + sk * (
                t[:, PAIR:] + gsum_in[1:2, at]
            )
            grad_k = jnp.where(rk[:, at].astype(F32) > 0.0, grad_k, 0.0)
            small[0, 1:2, at] = col_sum(grad_k)
            gk[:, at] = grad_k.astype(BF)
            grad_v = hid[:, at] + mm_nt(jnp.concatenate([kc, ks], axis=1), full)
            small[0, 2:3, at] = col_sum(grad_v)
            gv[:, at] = grad_v.astype(BF)
            return carry

        lax.fori_loop(0, PAIRS, back_remote, 0)
        weight_grad(K, tokt, gk)
        step(scatter[K])
        weight_grad(V, tokt, gv)
        step(scatter[V], scatter[Q], scatter[O], scatter[K])

        for j in range(width // TILE):
            at = pl.ds(j * TILE, TILE)
            total = acc[:, at] + mm_nt(gq[...], wq[at, :]) + mm_nt(gk[...], wk[at, :])
            in_out[1, :, at] = (total + mm_nt(gv[...], wv[at, :])).astype(BF)
        input_copy = local(in_out.at[1], out_input)
        input_copy.start()
        step(scatter[V], scatter[Q], scatter[O])

        norm_pair.wait()
        merged_pair.wait()

        def shard_grads(t, up_job, down_job, row):
            for j in range(shard // TILE):
                at = pl.ds(j * TILE, TILE)
                u = mm(nf[...], wu[t, :, at]) + ub[t, 0:1, at]
                value, slope = gelu_both(u)
                up_grad = mm_nt(mf[...], wd[t, at, :]) * slope
                small[0, row : row + 1, at] = col_sum(up_grad)
                act2[:, at] = value.astype(BF)
                upl2[:, at] = up_grad.astype(BF)
            for j in range(width // TILE):
                at = pl.ds(j * TILE, TILE)
                part_of(up_job)[pl.ds(j * TILE, TILE), :] = mm_tn(nf[:, at], upl2[...]).astype(BF)
            for j in range(shard // TILE):
                at = pl.ds(j * TILE, TILE)
                part_of(down_job)[pl.ds(j * TILE, TILE), :] = mm_tn(act2[:, at], mf[...]).astype(BF)

        shard_grads(across(2), UB, DB, 14)
        step(scatter[UB], scatter[DB])
        step(scatter[Q])
        step(z_first, scatter[V], scatter[K])
        shard_grads(mp, UA, DA, 15)
        step(scatter[UA], scatter[DA], smalls)
        step(z_first)
        step(scatter[UB], scatter[DB])
        step(scatter[V], scatter[K], z_second)
        step(scatter[UA], scatter[DA], smalls)
        step(z_first, gather[Q], gather[O])
        step(scatter[UB], scatter[DB], z_second)
        step(scatter[UA], scatter[DA], smalls)
        step(gather[Q], gather[O])
        step(z_second, gather[V], gather[K])
        step(scatter[UB], scatter[DB], ff_z)
        step(gather[Q], gather[O], smalls)
        step(gather[V], gather[K])
        step(scatter[UA], scatter[DA], ff_z, gather[UA], gather[DA])
        step(gather[Q], gather[O])
        step(gather[V], gather[K], smalls)
        step(gather[UA], gather[DA])
        step(gather[V], gather[K])
        step(gather[UA], gather[DA])
        step(gather[UA], gather[DA])
        for _ in smalls:
            pass
        for g in scatter + gather + [z_first, z_second, ff_z, smalls] + list(weight_jobs.values()):
            assert next(g, 1) == 1
        behind.finish()
        layer_copy.wait()
        input_copy.wait()
        for copy in final_copies:
            copy.wait()

    def call(*operands):
        vm = pltpu.VMEM
        big = lambda *s: vm(s, BF)
        flt = lambda *s: vm(s, F32)
        nsem = 224
        square = jax.ShapeDtypeStruct((width, width), BF)
        scratch = [
            big(rows, width), big(rows, width), big(width, width), big(width, width), big(width, width),
            big(width, width), flt(16, width),
            big(mp_size, width, shard), big(mp_size, shard, width), flt(mp_size, 8, shard),
            big(rows, width), big(rows, width), big(rows, width),
            flt(rows, 2 * rows), flt(rows, 2 * rows), flt(4, rows, 128),
            big(2 * rows, PAIR), big(2 * PAIR, PAIR), big(2 * rows, PAIR), big(rows, PAIR), big(4, 16, PAIR),
            flt(PAIRS, HD, 2 * PAIR), big(PAIRS, HD, 2 * PAIR), flt(8, width), flt(8, width),
            big(PAIRS, HD, 2 * PAIR), flt(8, width), big(PAIRS, HD, 2 * PAIR), flt(8, width),
            flt(8, width),
            flt(rows, width), flt(rows, width), big(rows, width), flt(rows, width), flt(rows, 128),
            flt(rows, width), big(2 * rows, width), big(2 * rows, width),
            big(mp_size, rows, shard), flt(mp_size, rows, shard), big(2 * rows, shard), big(2 * rows, shard),
            big(2, piece, width), flt(rows, width), flt(rows, width),
            big(rows, width), big(rows, width),
            big(rows, width), big(rows, width), big(rows, width),
            big(4 * width, width), big(6 * width, width),
            big(8, width // 2, width), big(8, width // 4, width), big(8, width // 8, width),
            big(8, max(1, nbits - nhalf), 16 if nbits == nhalf else piece, width), big(2, mp_size - 1, piece // 2, width),
            flt(nbits + 1, 16, width), flt(nbits, 16, width), flt(mp_size, 16, width),
            big(width, rows), big(2, rows, width),
            pltpu.SemaphoreType.DMA((32,)), pltpu.SemaphoreType.DMA((nsem,)), pltpu.SemaphoreType.DMA((nsem,)),
        ]
        spec = pl.BlockSpec(memory_space=pltpu.VMEM)
        anywhere = pl.BlockSpec(memory_space=pl.ANY)
        return pl.pallas_call(
            kernel,
            out_shape=(
                jax.ShapeDtypeStruct((rows, width), BF),
                jax.ShapeDtypeStruct((rows, width), BF),
                square, square, square, square, square, square,
                jax.ShapeDtypeStruct((16, width), F32),
            ),
            in_specs=[pl.BlockSpec(memory_space=pltpu.SMEM)] + [spec] * 10 + [anywhere] * 8,
            out_specs=(anywhere,) * 9,
            scratch_shapes=scratch,
            compiler_params=pltpu.CompilerParams(
                collective_id=0, has_side_effects=True, vmem_limit_bytes=63 * 1024 * 1024
            ),
        )(*operands)

    return call


def widen(layer, back, grads, small):
    rows, width = layer.shape
    steps = 8

    def kernel(*refs):
        n = len(grads)
        ins, outs = refs[: n + 3], refs[n + 3 :]
        outs[0][...] = ins[0][...]
        outs[1][...] = ins[1][...]
        for g in range(n):
            outs[2 + g][...] = ins[2 + g][...].astype(F32)

        @pl.when(pl.program_id(0) == 0)
        def _():
            for row, out in zip((0, 1, 2, 3, 4, 5, 15, 6, 7, 8), outs[2 + n :]):
                out[...] = ins[2 + n][row : row + 1, :].reshape(width)

    block = lambda x: pl.BlockSpec((x.shape[0] // steps, x.shape[1]), lambda i: (i, 0))
    whole = pl.BlockSpec(small.shape, lambda i: (0, 0))
    vector = pl.BlockSpec((width,), lambda i: (0,))
    mats = [layer, back, *grads]
    return pl.pallas_call(
        kernel,
        grid=(steps,),
        in_specs=[block(x) for x in mats] + [whole],
        out_specs=[block(x) for x in mats] + [vector] * 10,
        out_shape=[jax.ShapeDtypeStruct(x.shape, BF) for x in (layer, back)]
        + [jax.ShapeDtypeStruct(x.shape, F32) for x in grads]
        + [jax.ShapeDtypeStruct((width,), F32)] * 10,
        compiler_params=pltpu.CompilerParams(vmem_limit_bytes=62 * 1024 * 1024),
    )(*mats, small)


def solution(mesh):
    dp_size, mp_size = mesh.shape["dp"], mesh.shape["mp"]

    def on_device(
        tokens, doc_starts, query_proj, key_proj, value_proj, query_bias, key_bias, value_bias,
        output_proj, output_bias, attn_gain, attn_shift, up_proj, up_bias, down_proj, down_bias,
        ffn_gain, ffn_shift, cotangent,
    ):
        _, rows, width = tokens.shape
        shard = up_proj.shape[1]
        call = build(dp_size, mp_size, rows, width, shard)
        layer_out, input_grad, gq, gk, gv, go, gu, gd, small = call(
            doc_starts, query_bias, key_bias, value_bias, output_bias, attn_gain, attn_shift,
            down_bias, ffn_gain, ffn_shift, up_bias, tokens[0], cotangent[0],
            query_proj, key_proj, value_proj, output_proj, up_proj, down_proj,
        )
        layer_out, input_grad, gq, gk, gv, go, gu, gd, *vecs = widen(
            layer_out, input_grad, (gq, gk, gv, go, gu, gd), small
        )
        bq, bk, bv, bo, ga, sa, bu, bd, gf, sf = vecs
        return (
            layer_out[None], input_grad[None], gq, gk, gv, bq, bk, bv, go, bo, ga, sa,
            gu, bu, gd, bd, gf, sf,
        )

    rows_spec = P("dp", "mp", None)
    placed = (
        rows_spec, P("dp", None), P(), P(), P(), P(), P(), P(), P(), P(), P(), P(),
        P(None, "mp"), P("mp"), P("mp", None), P(), P(), P(), rows_spec,
    )
    results = (
        rows_spec, rows_spec, P(), P(), P(), P(), P(), P(), P(), P(), P(), P(),
        P(None, "mp"), P("mp"), P("mp", None), P(), P(), P(),
    )
    return jax.shard_map(
        on_device, mesh=mesh, in_specs=placed, out_specs=results, check_vma=False
    )
```

time: 249 us -> 178 us (0.71)
  Pallas kernels: 226 us -> 176 us
  local copies, waits for them, and re-layouts: 19.8 us -> 0 us
    pallas_call x1, Pallas kernels: 226 us -> 166 us  [call(): pl.pallas_call(kernel, out_shape=(jax.ShapeDtypeStruct((rows, width), BF)...]
    pallas_call x0 -> x1, Pallas kernels: none -> 10.2 us  [widen(): pl.pallas_call(kernel, grid=(steps,), in_specs=[block(x) for x in mats] +...]
    slice x2 -> x0, local copies, waits for them, and re-layouts: 10.1 us -> none  [the longest x1 8.37 us: on_device(): attn[3]]
    another operation x13 -> x0, local copies, waits for them, and re-layouts: 8.18 us -> none  [on_device(): jnp.stack([query_bias, key_bias, value_bias, output_bias, attn_gain, attn...]
where the time goes in v2:
time: 178 us; the launch traced here: 177 us
  Pallas kernels  176 us (99%)
    pallas_call x1, Pallas kernels, call(): pl.pallas_call(kernel, out_shape=(jax.ShapeDtypeStruct((rows, width), BF)...  166 us
    pallas_call x1, Pallas kernels, widen(): pl.pallas_call(kernel, grid=(steps,), in_specs=[block(x) for x in mats] +...  10.2 us

profile of v2, /device:TPU:0, one launch (start us, length us, event | category | flops | bytes accessed | tf_op | source)
XLA Modules:
  0.0 177.2 jit_solution(12222146176909976325)
XLA Ops:
  0.7 166.2 %shard_map.322 = (bf16[256,768]{1,0:T(8,128)(2,1)}, bf16[256,768]{1,0:T(8,128)(2,1)}, bf16[768,768]{1,0:T(8,128)(2,1)}, bf16[768,768]{1,0:T(8,128)(2,1)}, bf16[7...) custom-call(s32[1,2]{1,0:T(1,128)} %starts.1, ...), custom_call_target="tpu_custom_call" | custom-call | tf_op jit(solution)/shard_map/pallas_call | solution.py:862
  166.8 10.2 %shard_map.323 = (bf16[256,768]{1,0:T(8,128)(2,1)}, bf16[256,768]{1,0:T(8,128)(2,1)}, f32[768,768]{1,0:T(8,128)}, f32[768,768]{1,0:T(8,128)}, f32[768,768]{1,0:T...) custom-call(bf16[256,768]{1,0:T(8,128)(2,1)} %get-tuple-element.45.r, ...), custom_call_target="tpu_custom_call" | custom-call | tf_op jit(solution)/shard_map/pallas_call | solution.py:902

commit v3 on v2

--- a/solution.py
+++ b/solution.py
@@ -347,7 +347,7 @@
         norm_pair = remote(nf.at[pl.ds(0, rows)], nf.at[pl.ds(rows, rows)], neighbour)
         merged_pair = remote(mf.at[pl.ds(0, rows)], mf.at[pl.ds(rows, rows)], neighbour)
         pl.semaphore_wait(barrier, nbits + mp_size - 1)
-        pump(0)
+        pump(0, [1, 2])
         ahead.early()
         bias_copies = [remote(ub.at[mp], ub.at[mp], {"mp": across(i)}) for i in range(1, mp_size)]
         for copy in bias_copies:
@@ -372,9 +372,10 @@
         for c in range(CH):
             lax.fori_loop(c * PC, (c + 1) * PC, local_attention, 0)
             wave(c)
-            pump(1, [c + 1])
+            pump(0, [3]) if c == 0 else pump(1, [c])
             ahead.slot(c)
         wave(3)
+        pump(1, [3])
         ahead.slot(3)
         wave(4)
         ahead.slot(4)
@@ -736,8 +737,11 @@
 
         for c in range(CH):
             lax.fori_loop(c * PC, (c + 1) * PC, back_local, 0)
-            behind.service(c, behind.has_in)
-        step(scatter[O])
+            if c == 0:
+                step(scatter[O])
+            behind.slot(c)
+        behind.slot(3)
+        behind.slot(4)
         tokt[...] = tok[...].T
         weight_grad(Q, tokt, gq)
         step(scatter[Q])
@@ -880,7 +884,7 @@
 
 def widen(layer, back, grads, small):
     rows, width = layer.shape
-    steps = 8
+    steps = 2
 
     def kernel(*refs):
         n = len(grads)

time: 178 us -> 173 us (0.972)
  Pallas kernels: 176 us -> 171 us
    pallas_call x1, Pallas kernels: 166 us -> 163 us  [call(): pl.pallas_call(kernel, out_shape=(jax.ShapeDtypeStruct((rows, width), BF)...]
    pallas_call x1, Pallas kernels: 10.2 us -> 8.34 us  [widen(): pl.pallas_call(kernel, grid=(steps,), in_specs=[block(x) for x in mats] +...]
where the time goes in v3:
time: 173 us; the launch traced here: 172 us
  Pallas kernels  171 us (99%)
    pallas_call x1, Pallas kernels, call(): pl.pallas_call(kernel, out_shape=(jax.ShapeDtypeStruct((rows, width), BF)...  163 us
    pallas_call x1, Pallas kernels, widen(): pl.pallas_call(kernel, grid=(steps,), in_specs=[block(x) for x in mats] +...  8.34 us

profile of v3, /device:TPU:0, one launch (start us, length us, event | category | flops | bytes accessed | tf_op | source)
XLA Modules:
  0.0 172.3 jit_solution(14318980197281126697)
XLA Ops:
  0.7 163.2 %shard_map.322 = (bf16[256,768]{1,0:T(8,128)(2,1)}, bf16[256,768]{1,0:T(8,128)(2,1)}, bf16[768,768]{1,0:T(8,128)(2,1)}, bf16[768,768]{1,0:T(8,128)(2,1)}, bf16[7...) custom-call(s32[1,2]{1,0:T(1,128)} %starts.1, ...), custom_call_target="tpu_custom_call" | custom-call | tf_op jit(solution)/shard_map/pallas_call | solution.py:866
  163.8 8.3 %shard_map.323 = (bf16[256,768]{1,0:T(8,128)(2,1)}, bf16[256,768]{1,0:T(8,128)(2,1)}, f32[768,768]{1,0:T(8,128)}, f32[768,768]{1,0:T(8,128)}, f32[768,768]{1,0:T...) custom-call(bf16[256,768]{1,0:T(8,128)(2,1)} %get-tuple-element.45.r, ...), custom_call_target="tpu_custom_call" | custom-call | tf_op jit(solution)/shard_map/pallas_call | solution.py:906

commit v4 on v3

--- a/solution.py
+++ b/solution.py
@@ -398,7 +398,7 @@
         for j in range(width // TILE):
             at = pl.ds(j * TILE, TILE)
             hid[:, at] = tok[:, at].astype(F32) + mm(ctx[...], wo[:, at]) + vec[3:4, at]
-        RB = 64
+        RB = 128
 
         def first_norm(i, carry):
             at = pl.ds(pl.multiple_of(i * RB, RB), RB)
@@ -736,7 +736,7 @@
             return carry
 
         for c in range(CH):
-            lax.fori_loop(c * PC, (c + 1) * PC, back_local, 0)
+            lax.fori_loop(c * PC, (c + 1) * PC, back_local, 0, unroll=True)
             if c == 0:
                 step(scatter[O])
             behind.slot(c)

time: 173 us -> 172 us (level)
  no operation moved by 1% of the time
where the time goes in v4:
time: 172 us
  Pallas kernels  171 us (99%)
    pallas_call x1, Pallas kernels, call(): pl.pallas_call(kernel, out_shape=(jax.ShapeDtypeStruct((rows, width), BF)...  162 us
    pallas_call x1, Pallas kernels, widen(): pl.pallas_call(kernel, grid=(steps,), in_specs=[block(x) for x in mats] +...  8.34 us

profile of v4, /device:TPU:0, one launch (start us, length us, event | category | flops | bytes accessed | tf_op | source)
XLA Modules:
  0.0 171.5 jit_solution(4891483230528692538)
XLA Ops:
  0.7 162.4 %shard_map.322 = (bf16[256,768]{1,0:T(8,128)(2,1)}, bf16[256,768]{1,0:T(8,128)(2,1)}, bf16[768,768]{1,0:T(8,128)(2,1)}, bf16[768,768]{1,0:T(8,128)(2,1)}, bf16[7...) custom-call(s32[1,2]{1,0:T(1,128)} %starts.1, ...), custom_call_target="tpu_custom_call" | custom-call | tf_op jit(solution)/shard_map/pallas_call | solution.py:866
  163.0 8.3 %shard_map.323 = (bf16[256,768]{1,0:T(8,128)(2,1)}, bf16[256,768]{1,0:T(8,128)(2,1)}, f32[768,768]{1,0:T(8,128)}, f32[768,768]{1,0:T(8,128)}, f32[768,768]{1,0:T...) custom-call(bf16[256,768]{1,0:T(8,128)(2,1)} %get-tuple-element.45.r, ...), custom_call_target="tpu_custom_call" | custom-call | tf_op jit(solution)/shard_map/pallas_call | solution.py:906
